TPU v7x, 128 devices: a whole 4x4x4 slice. The times are simulated.
128 devices in a mesh: gz: 32 (over y, x, core), gy: 4 (over z).
Axes of the slice: x: 4, y: 4, z: 4, core: 2. Of those that a mesh axis runs over, the one named last changes fastest.
Arguments:
- volume: float32 [512, 512, 512], P('gz', 'gy'), may hold values from -6 to 6
- labels: int32 [512, 512, 512], P('gz', 'gy'), may hold values from 0 to 3
- patch_list: int32 [32, 4, 256], P('gz', 'gy'), may hold values from -1 to 255, as said below
- stem_kernel: float32 [3, 3, 3], replicated, may hold values from -1.25 to 1.25
- embed_weight: bfloat16 [4096, 1024], replicated, may hold values from -0.09375 to 0.09375
- norm_gain: float32 [2, 1024], replicated, may hold values from 0.1 to 1.9
- up_weight: bfloat16 [2, 1024, 4096], P(None, None, 'gy'), may hold values from -0.1875 to 0.1875
- down_weight: bfloat16 [2, 4096, 1024], P(None, 'gy'), may hold values from -0.09375 to 0.09375
- head_weight: bfloat16 [1024, 256], replicated, may hold values from -0.1875 to 0.1875
- skip_weight: float32 [4], replicated, may hold values from -3 to 3
- class_bias: float32 [4], replicated, may hold values from -3 to 3
Outputs:
- patch_dice: float32 [32, 4, 4, 256], P('gz', 'gy')
- dice: float32 [4], replicated
Inputs may be any that keep to these rules, and one draw needn't show every extreme that they name: `patch_list`: each device block's row lists the numbers of its listed patches, each once and ascending, followed by -1 in the remaining slots; over all blocks exactly 20480 patches are listed, and some block lists all 256 of its patches.
All inputs are finite; a program needn't handle non-finite values.
Results may differ from a plain program's by a relative error of at most 0.0008.
Values may be sent and summed in bfloat16 or wider, within the bound.
A program may use at most 256 MiB of HBM per device.

v0:
```python
from functools import partial

import jax
import jax.numpy as jnp
from jax import lax
from jax.sharding import PartitionSpec as P

EPS = 1e-05


def padded_2(x, sides, width):
    for axis, dim in sides:
        count, length = (lax.axis_size(axis), x.shape[dim])
        up = [(i, (i + 1) % count) for i in range(count - 1)]
        down = [(j, i) for i, j in up]
        last = lax.slice_in_dim(x, length - width, length, axis=dim)
        first = lax.slice_in_dim(x, 0, width, axis=dim)
        before = lax.ppermute(last, axis, up)
        after = lax.ppermute(first, axis, down)
        x = jnp.concatenate([before, x, after], axis=dim)
    return x


def carried_in(value, axis, join, neutral):
    count, mine = (lax.axis_size(axis), lax.axis_index(axis))
    pieces = lax.all_gather(value, axis)
    so_far = jnp.full_like(value, 0) + jnp.asarray(neutral, value.dtype)

    def turn(position, so_far):
        longer = join(so_far, pieces[position])
        return jnp.where(position < mine, longer, so_far)

    return lax.fori_loop(0, count - 1, turn, so_far)


def stem_field(padded, stem_kernel, shape):
    depth, rows, cols = shape
    total = jnp.zeros(shape, jnp.float32)
    for first in range(3):
        for second in range(3):
            for third in range(3):
                total = (
                    total
                    + stem_kernel[first, second, third]
                    * padded[first : first + depth, second : second + rows, third : third + cols]
                )
    return jax.nn.silu(total).astype(jnp.bfloat16)


def patch_layout(field, edge):
    depth, rows, cols = field.shape
    shaped = field.reshape(edge, rows // edge, edge, cols // edge, edge)
    return shaped.transpose(1, 3, 0, 2, 4).reshape(
        rows // edge * (cols // edge), edge * edge * edge
    )


def normalize(rows, gain):
    values = rows.astype(jnp.float32)
    centre = jnp.mean(values, -1, keepdims=True)
    centred = values - centre
    spread = jnp.mean(centred * centred, -1, keepdims=True)
    return (centred * lax.rsqrt(spread + EPS) * gain).astype(jnp.bfloat16)


def block_rows(piece, start, gain, up_matrix, down_matrix):
    normed = normalize(piece, gain)
    upper = jnp.dot(normed, up_matrix, preferred_element_type=jnp.float32)
    active = jax.nn.gelu(upper, approximate=True).astype(jnp.bfloat16)
    part = jnp.dot(active, down_matrix, preferred_element_type=jnp.float32)
    return lax.optimization_barrier(part.astype(jnp.bfloat16)).astype(jnp.float32)


def add_counts(earlier, later):
    return earlier + later


def expand_blocks(coarse, classes, edge):
    lead = coarse.shape[:-1]
    grid = coarse.reshape(lead + (classes, 4, 1, 4, 1, 4, 1))
    grid = jnp.broadcast_to(grid, lead + (classes, 4, edge, 4, edge, 4, edge))
    return grid.reshape(lead + (classes, 64 * edge * edge * edge))


def patch_terms(coarse_vox, stem_rows, label_rows, skip_weight, class_bias):
    classes = skip_weight.shape[0]
    logits = (
        coarse_vox
        + skip_weight[:, None] * stem_rows.astype(jnp.float32)[..., None, :]
        + class_bias[:, None]
    )
    probs = jax.nn.sigmoid(logits)
    numbers = jnp.arange(classes, dtype=jnp.int32)
    match = (label_rows[..., None, :] == numbers[:, None]).astype(jnp.float32)
    return (jnp.sum(probs * match, -1), jnp.sum(probs, -1), jnp.sum(match, -1))


def per_device(
    volume,
    labels,
    patch_list,
    stem_kernel,
    embed_weight,
    norm_gain,
    up_weight,
    down_weight,
    head_weight,
    skip_weight,
    class_bias,
):
    edge = volume.shape[0]
    classes = skip_weight.shape[0]
    padded = padded_2(volume.astype(jnp.bfloat16), (("gz", 0), ("gy", 1)), 1).astype(volume.dtype)
    padded = jnp.pad(padded, ((0, 0), (0, 0), (1, 1)))
    stem = stem_field(padded, stem_kernel, volume.shape)
    stem_rows = patch_layout(stem, edge)
    label_rows = patch_layout(labels, edge)
    slots = patch_list[0, 0]
    patch_dev = slots.shape[0]
    keep = patch_dev * 5 // 8
    depth_devs = lax.axis_size("gz")
    row_devs = lax.axis_size("gy")
    devices = depth_devs * row_devs
    cap = (patch_dev + devices - 1) // devices
    listed = slots >= 0
    count = jnp.sum(listed.astype(jnp.int32))
    offset = carried_in(count, ("gz", "gy"), add_counts, jnp.int32(0))
    position = jnp.arange(patch_dev, dtype=jnp.int32)
    ranks = offset + position
    send_at = ranks % devices * cap + position // devices
    owner_slot = jnp.where(listed, ranks // devices, -1).astype(jnp.int32)
    safe_slot = jnp.maximum(slots, 0)
    tokens = stem_rows[safe_slot]
    payload = tokens
    payload = jnp.where(listed[:, None], payload, jnp.zeros((), payload.dtype))
    outgoing = jnp.zeros((devices * cap, payload.shape[1]), payload.dtype).at[send_at].set(payload)
    outgoing_ids = jnp.full((devices * cap,), -1, jnp.int32).at[send_at].set(owner_slot)
    arrived, arrived_ids = (
        lax.all_to_all(
            outgoing.reshape(devices, cap, payload.shape[1]),
            ("gz", "gy"),
            split_axis=0,
            concat_axis=0,
            tiled=True,
        ),
        lax.all_to_all(
            outgoing_ids.reshape(devices, cap),
            ("gz", "gy"),
            split_axis=0,
            concat_axis=0,
            tiled=True,
        ),
    )
    arrived = arrived.reshape(devices * cap, payload.shape[1])
    arrived_ids = arrived_ids.reshape(devices * cap)
    valid_ids = arrived_ids >= 0
    place = jnp.where(valid_ids, arrived_ids, keep)
    owned = jnp.zeros((keep, arrived.shape[1]), arrived.dtype).at[place].set(arrived, mode="drop")
    hidden = jnp.dot(owned, embed_weight, preferred_element_type=jnp.float32).astype(jnp.bfloat16)
    for layer in range(norm_gain.shape[0]):
        work = partial(
            block_rows,
            gain=norm_gain[layer],
            up_matrix=up_weight[layer],
            down_matrix=down_weight[layer],
        )
        partial_sums = work(lax.all_gather(hidden, "gy", axis=0, tiled=True), jnp.int32(0))
        mlp_sum = lax.psum_scatter(
            partial_sums.astype(jnp.bfloat16), "gy", scatter_dimension=0, tiled=True
        ).astype(jnp.float32)
        hidden = (hidden.astype(jnp.float32) + mlp_sum).astype(jnp.bfloat16)
    back = jnp.where(
        valid_ids[:, None], hidden[jnp.maximum(arrived_ids, 0)], jnp.zeros((), hidden.dtype)
    )
    width = back.shape[1]
    returned = lax.all_to_all(
        back.reshape(devices, cap, width), ("gz", "gy"), split_axis=0, concat_axis=0, tiled=True
    )
    mine = returned.reshape(devices * cap, width)[send_at]
    coarse = jnp.dot(mine, head_weight, preferred_element_type=jnp.float32).astype(jnp.bfloat16)
    coarse = jnp.where(listed[:, None], coarse, jnp.zeros((), coarse.dtype))
    selector = (slots[None, :] == position[:, None]).astype(jnp.bfloat16)
    patch_coarse = jnp.dot(selector, coarse, preferred_element_type=jnp.float32)
    inter, mass, count_c = patch_terms(
        expand_blocks(patch_coarse, classes, edge // 4),
        stem_rows,
        label_rows,
        skip_weight,
        class_bias,
    )
    patch_dice = ((2.0 * inter + 1.0) / (mass + count_c + 1.0)).T[None, None]
    totals = lax.psum((jnp.sum(inter, 0), jnp.sum(mass, 0), jnp.sum(count_c, 0)), ("gz", "gy"))
    dice = (2.0 * totals[0] + 1.0) / (totals[1] + totals[2] + 1.0)
    return (patch_dice, dice)


def solution(mesh):
    placed = (
        P("gz", "gy", None),
        P("gz", "gy", None),
        P("gz", "gy", None),
        P(),
        P(),
        P(),
        P(None, None, "gy"),
        P(None, "gy", None),
        P(),
        P(),
        P(),
    )
    return jax.shard_map(
        per_device,
        mesh=mesh,
        in_specs=placed,
        out_specs=(P("gz", "gy", None, None), P()),
        check_vma=False,
    )
```

profile of v0, /device:TPU:1, one launch (start us, length us, event | category | flops | bytes accessed | tf_op | source)
XLA Modules:
  0.0 749.3 jit_solution(7555420219223095452)
XLA Ops:
  9.5 68.6 %all-reduce.1 = s32[128]{0:T(128)S(1)} all-reduce(s32[128]{0:T(128)S(1)} %dynamic-update-slice), channel_id=1, replica_groups=mesh['gz'=32,'gy'=4] {'gz','gy'}, use_global_device_ids=true, to_apply=%add.1 | all-reduce | flops 128 | bytes 1024
  78.1 149.0 %while.13 = (s32[]{:T(128)}, s32[]{:T(128)}, s32[]{:T(128)}, s32[128]{0:T(128)S(1)}, s32[]{:T(128)}) while((s32[]{:T(128)}, s32[]{:T(128)}, s32[]{:T(128)}, s32[128]{0:T(128)S(1)}, s32[]{:T(128)}) %tuple.66), condition=%wide.region_2.3_spmd, body=%wide.region_1.2_spmd.sunk | while | flops 5 | bytes 115 | solution.py:33
  229.3 4.7 all-to-all-start
  236.5 3.5 collective-permute-start
  246.4 3.2 collective-permute-start.2
  255.3 39.5 %multiply_convert_fusion = bf16[16,128,512]{2,1,0:T(8,128)(2,1)S(1)} fusion(f32[18,130,512]{2,1,0:T(8,128)S(1)} %maximum_convert_fusion, f32[]{:T(128)} %bitcast.34, f32[]{:T(128)} %bitcast.33, f32[]{:T(128)} %bitcast.32, f32[]{:T(128)} %bitcast.31, f32[]{:T(128)} %bitcast.30, f32[]{:T(128)} %bitcast.29, f32[]{:T(128)} %bitcast.28, f32[]{:T(128)} %bitcast.27, ...), kind=kLoop, calls=%fused_computation.88 | loop fusion | flops 60817408 | bytes 44859500 | tf_op jit(solution)/shard_map/convert_element_type | solution.py:47
  294.8 15.4 %reshape.239 = bf16[16,8,16,32,16]{4,3,2,1,0:T(8,128)(2,1)} reshape(bf16[16,128,512]{2,1,0:T(8,128)(2,1)S(1)} %multiply_convert_fusion) | data formatting | bytes 4194304 | tf_op jit(solution)/shard_map/reshape | solution.py:52
  310.2 16.3 %copy.60 = bf16[8,32,16,16,16]{1,0,4,3,2:T(8,128)(2,1)} copy(bf16[8,32,16,16,16]{4,1,3,0,2:T(8,128)(2,1)} %bitcast.98) | data formatting | bytes 4194304 | tf_op jit(solution)/shard_map/transpose | solution.py:53
  326.5 9.7 %reshape.240 = bf16[256,4096]{0,1:T(8,128)(2,1)S(1)} reshape(bf16[8,32,16,16,16]{1,0,4,3,2:T(8,128)(2,1)} %copy.60) | data formatting | bytes 4194304 | tf_op jit(solution)/shard_map/reshape | solution.py:53
  339.2 10.8 %scatter_custom_fusion.1 = bf16[256,4096]{1,0:T(8,128)(2,1)S(1)} fusion(s32[256]{0:T(256)S(1)} %bitcast.107, pred[256]{0:T(512)(128)(4,1)S(1)} %get-tuple-element.99, bf16[]{:T(256)} %constant.105.clone.1, bf16[256,4096]{1,0:T(8,128)(2,1)} %copy.61, s32[1024]{0:T(1024)S(1)} %pad_clamp_fusion.2), kind=kCustom, calls=%fused_computation.135 | custom fusion | flops 1048576 | bytes 4199936 | tf_op jit(solution)/shard_map/scatter | solution.py:136
  352.7 13.5 %all-to-all-start.1 = ((bf16[128,2,4096]{2,1,0:T(2,128)(2,1)}), bf16[128,2,4096]{2,1,0:T(2,128)(2,1)S(1)}, u32[]{:S(2)}, u32[]{:S(2)}) async-start(bf16[128,2,4096]{2,1,0:T(2,128)(2,1)} %reshape.241), calls=%async_computation.1 | async-start | bytes 4194304 | tf_op jit(solution)/shard_map/all_to_all | solution.py:139
  367.7 29.0 %all-to-all-done.1 = bf16[128,2,4096]{2,1,0:T(2,128)(2,1)S(1)} async-done(((bf16[128,2,4096]{2,1,0:T(2,128)(2,1)}), bf16[128,2,4096]{2,1,0:T(2,128)(2,1)S(1)}, u32[]{:S(2)}, u32[]{:S(2)}) %all-to-all-start.1) | async-done | bytes 2097184 | tf_op jit(solution)/shard_map/all_to_all | solution.py:139
  399.0 4.7 scatter_custom_fusion.2
  403.8 5.6 convolution_convert_fusion
  409.5 19.4 %all-gather.3.cloned.1.call-done = bf16[640,1024]{1,0:T(8,128)(2,1)} async-done(((bf16[160,1024]{1,0:T(8,128)(2,1)}), bf16[640,1024]{1,0:T(8,128)(2,1)}) %all-gather.3.cloned.1.call-update) | async-done | bytes 1310736 | tf_op jit(solution)/shard_map/all_gather | solution.py:167
  432.3 6.7 fusion.88
  439.1 25.2 %reduce-scatter.3.cloned.1.call-done = bf16[160,1024]{1,0:T(8,128)(2,1)} async-done(((bf16[640,1024]{1,0:T(8,128)(2,1)}), bf16[160,1024]{1,0:T(8,128)(2,1)}) %reduce-scatter.3.cloned.1.call-update) | async-done | bytes 327696 | tf_op jit(solution)/shard_map/reduce_scatter | solution.py:168
  466.6 24.4 %all-gather.5.cloned.1.call-done = bf16[640,1024]{1,0:T(8,128)(2,1)} async-done(((bf16[160,1024]{1,0:T(8,128)(2,1)}), bf16[640,1024]{1,0:T(8,128)(2,1)}) %all-gather.5.cloned.1.call-update) | async-done | bytes 1310736 | tf_op jit(solution)/shard_map/all_gather | solution.py:167
  494.4 6.7 fusion.91
  501.1 19.8 %reshape.237 = s32[16,8,16,32,16]{4,3,2,1,0:T(8,128)} reshape(s32[16,128,512]{2,1,0:T(8,128)} %param.14) | data formatting | bytes 8388608 | tf_op jit(solution)/shard_map/reshape | solution.py:52
  520.9 24.6 %copy.55 = s32[8,32,16,16,16]{1,0,4,3,2:T(8,128)} copy(s32[8,32,16,16,16]{4,1,3,0,2:T(8,128)} %bitcast.99) | data formatting | bytes 8388608 | tf_op jit(solution)/shard_map/transpose | solution.py:53
  545.5 12.2 %eq.50 = s32[256,4096]{0,1:T(8,128)} reshape(s32[8,32,16,16,16]{1,0,4,3,2:T(8,128)} %copy.55) | data formatting | bytes 8388608 | tf_op jit(solution)/shard_map/eq | solution.py:94
  557.7 12.6 %eq.42 = s32[256,4,4,4,4,4,4]{0,6,5,4,3,2,1:T(4,128)} reshape(s32[8,32,16,16,16]{1,0,4,3,2:T(8,128)} %copy.55) | data formatting | bytes 8388608 | tf_op jit(solution)/shard_map/eq | solution.py:94
  570.3 5.6 copy.64
  575.9 5.0 convert_reduce_fusion
  581.2 16.0 %copy.59 = bf16[16,8,16,32,16]{3,4,2,0,1:T(8,128)(2,1)} copy(bf16[16,8,16,32,16]{4,3,2,1,0:T(8,128)(2,1)} %reshape.239) | data formatting | bytes 4194304 | tf_op jit(solution)/shard_map/reshape | solution.py:52
  601.0 9.9 %all-to-all-start.2 = ((bf16[128,2,1024]{2,1,0:T(2,128)(2,1)}), bf16[128,2,1024]{2,1,0:T(2,128)(2,1)S(1)}, u32[]{:S(2)}, u32[]{:S(2)}) async-start(bf16[128,2,1024]{2,1,0:T(2,128)(2,1)} %broadcast_select_fusion.2), calls=%async_computation.4 | async-start | bytes 1048576 | tf_op jit(solution)/shard_map/all_to_all | solution.py:176
  610.9 11.5 %bitcast_convert_fusion = f32[8,32,16,16,16]{1,4,3,2,0:T(8,128)} fusion(bf16[16,8,16,32,16]{3,4,2,0,1:T(8,128)(2,1)} %copy.59), kind=kLoop, calls=%fused_computation.32 | loop fusion | flops 1048576 | bytes 6291456 | tf_op jit(solution)/shard_map/convert_element_type | solution.py:89
  622.3 17.7 %copy.62 = f32[8,32,16,16,16]{1,0,4,3,2:T(8,128)} copy(f32[8,32,16,16,16]{1,4,3,2,0:T(8,128)} %bitcast_convert_fusion) | data formatting | bytes 8388608 | tf_op jit(solution)/shard_map/convert_element_type | solution.py:89
  640.0 12.6 %reshape.244 = f32[256,4,4,4,4,4,4]{0,6,5,4,3,2,1:T(4,128)} reshape(f32[8,32,16,16,16]{1,0,4,3,2:T(8,128)} %copy.62) | data formatting | bytes 8388608 | tf_op jit(solution)/shard_map/convert_element_type | solution.py:89
  654.7 19.5 %fusion.1 = (f32[4]{0:T(128)S(1)}, f32[256,4]{0,1:T(4,128)S(1)}, f32[256,4]{0,1:T(4,128)S(1)}, f32[4]{0:T(128)S(1)}) fusion(s32[256,4,4,4,4,4,4]{0,6,5,4,3,2,1:T(4,128)} %eq.42, f32[4]{0:T(128)S(1)} %copy-done.6, f32[256,4,4,4,4,4,4]{0,6,5,4,3,2,1:T(4,128)} %reshape.244, f32[4]{0:T(128)S(1)} %copy-done.7, f32[256,4,4,4,4]{0,4,3,2,1:T(4,128)S(1)} %broadcast_in_dim.82), kind=kLoop, calls=%fused_computation.12 | loop fusion | flops 50329592 | bytes 8659008 | tf_op jit(solution)/shard_map/reduce_sum | solution.py:192
  674.3 67.2 %all-reduce.2 = (f32[4]{0:T(128)S(1)}, f32[4]{0:T(128)S(1)}) all-reduce(f32[4]{0:T(128)S(1)} %add.334, f32[4]{0:T(128)S(1)} %get-tuple-element.82), channel_id=1, replica_groups=mesh['gz'=32,'gy'=4] {'gz','gy'}, use_global_device_ids=true, to_apply=%region_18.19 | all-reduce | flops 8 | bytes 64 | tf_op jit(solution)/shard_map/psum | solution.py:192
  (208 shorter events, 118.2 us)
Async XLA Ops:
  7.2 646.9 %copy-start = (bf16[1024,256]{1,0:T(8,128)(2,1)S(1)}, bf16[1024,256]{1,0:T(8,128)(2,1)}, u32[]{:S(2)}) copy-start(bf16[1024,256]{1,0:T(8,128)(2,1)} %param.21) | copy-start | bytes 1572868
  7.2 234.8 %copy-start.5 = (s32[1,1,256]{2,1,0:T(1,128)S(1)}, s32[1,1,256]{2,1,0:T(1,128)}, u32[]{:S(2)}) copy-start(s32[1,1,256]{2,1,0:T(1,128)} %param.15) | copy-start | bytes 3076
  7.2 234.8 %copy-start.3 = (f32[3,3,3]{2,1,0:T(4,128)S(1)}, f32[3,3,3]{2,1,0:T(4,128)}, u32[]{:S(2)}) copy-start(f32[3,3,3]{2,1,0:T(4,128)} %param.16) | copy-start | bytes 328
  229.3 123.4 %all-to-all-start = ((s32[128,1,2]{2,1,0:T(1,128)}), s32[128,1,2]{2,1,0:T(1,128)S(1)}, u32[]{:S(2)}, u32[]{:S(2)}) async-start(s32[128,1,2]{2,1,0:T(1,128)} %bitcast.5), calls=%async_computation | async-start | bytes 131072 | tf_op jit(solution)/shard_map/all_to_all | solution.py:146
  236.5 6.9 collective-permute-start
  240.0 6.3 collective-permute-start.1
  246.4 4.7 collective-permute-start.2
  249.6 4.7 collective-permute-start.3
  352.7 44.1 %all-to-all-start.1 = ((bf16[128,2,4096]{2,1,0:T(2,128)(2,1)}), bf16[128,2,4096]{2,1,0:T(2,128)(2,1)S(1)}, u32[]{:S(2)}, u32[]{:S(2)}) async-start(bf16[128,2,4096]{2,1,0:T(2,128)(2,1)} %reshape.241), calls=%async_computation.1 | async-start | bytes 4194304 | tf_op jit(solution)/shard_map/all_to_all | solution.py:139
  366.2 62.7 %all-gather.3.cloned.1.call-start = ((), (), s32[]{:S(2)}) async-start(), calls=%async_computation.5 | async-start | bytes 1638400 | tf_op jit(solution)/shard_map/all_gather | solution.py:167
  403.7 5.7 copy-start.4
  409.4 54.9 %reduce-scatter.3.cloned.1.call-start = ((), (), s32[]{:S(2)}) async-start(), calls=%async_computation.6 | async-start | bytes 1638400 | tf_op jit(solution)/shard_map/reduce_scatter | solution.py:168
  432.3 32.0 %copy-start.2 = (bf16[160,1024]{1,0:T(8,128)(2,1)S(1)}, bf16[160,1024]{1,0:T(8,128)(2,1)}, u32[]{:S(2)}) copy-start(bf16[160,1024]{1,0:T(8,128)(2,1)} %convolution_convert_fusion) | copy-start | bytes 983044
  439.0 52.0 %all-gather.5.cloned.1.call-start = ((), (), s32[]{:S(2)}) async-start(), calls=%async_computation.7 | async-start | bytes 1638400 | tf_op jit(solution)/shard_map/all_gather | solution.py:167
  466.1 131.0 %reduce-scatter.5.cloned.1.call-start = ((), (), s32[]{:S(2)}) async-start(), calls=%async_computation.8 | async-start | bytes 1638400 | tf_op jit(solution)/shard_map/reduce_scatter | solution.py:168
  581.2 16.0 %copy-start.1 = (bf16[160,1024]{1,0:T(8,128)(2,1)S(1)}, bf16[160,1024]{1,0:T(8,128)(2,1)}, u32[]{:S(2)}) copy-start(bf16[160,1024]{1,0:T(8,128)(2,1)} %add_convert_fusion.1) | copy-start | bytes 983044
  601.0 51.7 %all-to-all-start.2 = ((bf16[128,2,1024]{2,1,0:T(2,128)(2,1)}), bf16[128,2,1024]{2,1,0:T(2,128)(2,1)S(1)}, u32[]{:S(2)}, u32[]{:S(2)}) async-start(bf16[128,2,1024]{2,1,0:T(2,128)(2,1)} %broadcast_select_fusion.2), calls=%async_computation.4 | async-start | bytes 1048576 | tf_op jit(solution)/shard_map/all_to_all | solution.py:176
  652.6 2.1 copy-start.6
  652.7 2.1 copy-start.7
Sparse Core Ops, SparseCore 0:
  409.5 19.3 all-gather.2
  439.1 25.1 reduce-scatter.2
  466.2 24.7 all-gather.4
  501.2 25.0 reduce-scatter.4
where the time goes:
time: 757 us; the launch traced here: 749 us
  local copies, waits for them, and re-layouts  257 us (34%)
  blocking collectives  136 us (18%)
  other arithmetic  104 us (14%)
  waiting for transfers between devices  104 us (14%)
  loops' own time  75.4 us (10%)
  starting transfers between devices  38.8 us (5%)
  matrix products  19.5 us (3%)
  between operations  14.3 us (2%)
    another operation x1, loops' own time, carried_in(): return lax.fori_loop(0, count - 1, turn, so_far)  75.4 us
    dynamic_slice x127, local copies, waits for them, and re-layouts, turn(): longer = join(so_far, pieces[position])  73.6 us
    unnamed x1, blocking collectives  68.6 us
    psum x1, blocking collectives, per_device(): lax.psum((jnp.sum(inter, 0), jnp.sum(mass, 0), jnp.sum(count_c, 0)), ('gz...  67.2 us
    reshape x3, local copies, waits for them, and re-layouts, patch_layout(): shaped = field.reshape(edge, rows // edge, edge, cols // edge, edge)  51.2 us
    all_gather x2, waiting for transfers between devices, per_device(): lax.all_gather(hidden, 'gy', axis=0, tiled=True)  43.9 us
    transpose x2, local copies, waits for them, and re-layouts, patch_layout(): shaped.transpose(1, 3, 0, 2, 4)  40.9 us
    convert_element_type x1, other arithmetic, stem_field(): return jax.nn.silu(total).astype(jnp.bfloat16)  39.5 us
  transfers between devices with their start and end apart: 11, of which 6 were waited for; matrix products, arithmetic and copies ran while one was open for 32% of the time, Pallas kernels for 0%

commit v1 on v0

v1 whole, which is shorter than its diff:
```python
import jax
import jax.numpy as jnp
from jax import lax
from jax.experimental import pallas as pl
from jax.experimental.pallas import tpu as pltpu
from jax.sharding import PartitionSpec as P

EPS = 1e-05
MESH = pl.DeviceIdType.MESH
F32 = jnp.float32
BF16 = jnp.bfloat16

NEAR, FAR, HALF = 128, 512, 64


def kernel(
    vol, lab, slots, taps, emb, gain, up, down, head, skip, bias,
    out,
    pad, wts, embuf, stem, labels, lhs, xacc, xn, hid, coarse, upq, expand, sums, headbuf, gainbuf,
    hs, hr, cs, cr, vsem, labsem, z1s, z1r, z2s, z2r, a1s, a1r, a2s, a2r, ss, sr, lsem,
):
    gz, gy = lax.axis_index("gz"), lax.axis_index("gy")
    core = lax.rem(gz, 2)
    chip = lax.div(gz, 2)
    cx, cy = lax.rem(chip, 4), lax.div(chip, 4)
    seed = (1 - core) * cx + core * cy

    def along(step):
        first = (cy * 4 + lax.rem(cx + step, 4)) * 2
        second = (lax.rem(cy + step, 4) * 4 + cx) * 2 + 1
        return ((1 - core) * first + core * second, gy)

    z_next, z_prev = (gz, lax.rem(gy + 1, 4)), (gz, lax.rem(gy + 3, 4))
    a_next, a_prev = along(1), along(3)
    g_next, g_prev = (lax.rem(gz + 1, 32), gy), (lax.rem(gz + 31, 32), gy)
    twin = (gz + 1 - 2 * core, gy)
    q_prev, q_next, q_far = lax.rem(gy + 3, 4), lax.rem(gy + 1, 4), lax.rem(gy + 2, 4)
    foreign = (q_prev, q_next, q_far)

    barrier = pltpu.get_barrier_semaphore()
    for peer in (z_next, z_prev, a_next, a_prev, g_next, g_prev, twin):
        pl.semaphore_signal(barrier, inc=1, device_id=peer, device_id_type=MESH)
    pl.semaphore_wait(barrier, 7)

    def remote(src, dst, send, recv, peer):
        return pltpu.make_async_remote_copy(
            src_ref=src, dst_ref=dst, send_sem=send, recv_sem=recv, device_id=peer, device_id_type=MESH
        )

    sent = []

    def send(*args):
        copy = remote(*args)
        copy.start()
        sent.append(copy)

    def landed(dst, send_sem, recv_sem, peer):
        remote(dst, dst, send_sem, recv_sem, peer).wait_recv()

    body = pl.ds(8, 128)
    inner = pl.ds(1, 16)
    above, below = pl.ds(0, 8), pl.ds(136, 8)
    blocks = [pl.ds(cb * 128, 128) for cb in range(4)]
    for cb, cols in enumerate(blocks):
        send(vol.at[15, :, cols], pad.at[0, cb, body], hs.at[0, cb], hr.at[0, cb], g_next)
        send(vol.at[0, :, cols], pad.at[17, cb, body], hs.at[1, cb], hr.at[1, cb], g_prev)
    for cb, cols in enumerate(blocks):
        send(vol.at[:, pl.ds(120, 8), cols], pad.at[inner, cb, above], hs.at[2, cb], hr.at[2, cb], z_next)
        send(vol.at[:, pl.ds(0, 8), cols], pad.at[inner, cb, below], hs.at[3, cb], hr.at[3, cb], z_prev)

    groups = (4, 8, 12, 0)
    local = []
    parts = ((3, 6), (9, 4), (13, 3), (0, 3))
    for n, (first, many) in enumerate(parts):
        for cb, cols in enumerate(blocks):
            copy = pltpu.make_async_copy(
                vol.at[pl.ds(first, many), :, cols], pad.at[pl.ds(1 + first, many), cb, body], vsem.at[n, cb]
            )
            copy.start()
            local.append(copy)

    def volume_wait(n):
        for copy in local[n * 4 : n * 4 + 4]:
            copy.wait()

    def embed_copy(g):
        return pltpu.make_async_copy(
            emb.at[pl.ds(groups[g] * 256, 1024)], embuf.at[g % 2], lsem.at[4 + g % 2]
        )

    embed_copy(0).start()

    def own(t):
        return (up, down)[t % 2].at[t // 2]

    def rows(which, at, offset=0, size=NEAR):
        return pl.ds(which * FAR + at * NEAR + offset, size)

    def near(t, q, at):
        return wts.at[t // 2, t % 2, q, rows(core, at)]

    def half(t, q, at, h):
        return wts.at[t // 2, t % 2, q, rows(core, at, h * HALF, HALF)]

    seed_prev, seed_next, seed_far = lax.rem(seed + 3, 4), lax.rem(seed + 1, 4), lax.rem(seed + 2, 4)

    def step_z1(t):
        piece = own(t).at[rows(core, seed)]
        send(piece, near(t, gy, seed), z1s.at[t, 0], z1r.at[t, 0], z_next)
        send(piece, near(t, gy, seed), z1s.at[t, 1], z1r.at[t, 1], z_prev)

    def spread(t, n):
        piece = near(t, foreign[n], seed)
        send(piece, piece, a1s.at[t, n, 0], a1r.at[t, n, 0], a_next)
        send(piece, piece, a1s.at[t, n, 1], a1r.at[t, n, 1], a_prev)

    def step_b(t):
        landed(near(t, q_prev, seed), z1s.at[t, 0], z1r.at[t, 0], z_prev)
        piece = half(t, q_prev, seed, 0)
        send(piece, piece, z2s.at[t, 0], z2r.at[t, 0], z_next)
        spread(t, 0)
        landed(near(t, q_next, seed), z1s.at[t, 1], z1r.at[t, 1], z_next)
        piece = half(t, q_next, seed, 1)
        send(piece, piece, z2s.at[t, 1], z2r.at[t, 1], z_prev)
        spread(t, 1)

    def step_c(t):
        landed(half(t, q_far, seed, 0), z2s.at[t, 0], z2r.at[t, 0], z_prev)
        landed(half(t, q_far, seed, 1), z2s.at[t, 1], z2r.at[t, 1], z_next)
        spread(t, 2)

    def step_d(t, n):
        q = foreign[n]
        landed(near(t, q, seed_prev), a1s.at[t, n, 0], a1r.at[t, n, 0], a_prev)
        piece = half(t, q, seed_prev, 0)
        send(piece, piece, a2s.at[t, n, 0], a2r.at[t, n, 0], a_next)
        landed(near(t, q, seed_next), a1s.at[t, n, 1], a1r.at[t, n, 1], a_next)
        piece = half(t, q, seed_next, 1)
        send(piece, piece, a2s.at[t, n, 1], a2r.at[t, n, 1], a_prev)

    def step_e(t, n):
        q = foreign[n]
        landed(half(t, q, seed_far, 0), a2s.at[t, n, 0], a2r.at[t, n, 0], a_prev)
        landed(half(t, q, seed_far, 1), a2s.at[t, n, 1], a2r.at[t, n, 1], a_next)
        piece = wts.at[t // 2, t % 2, q, pl.ds(core * FAR, FAR)]
        send(piece, piece, ss.at[t, n], sr.at[t, n], twin)

    def step_f(t, n):
        dst = wts.at[t // 2, t % 2, foreign[n], pl.ds((1 - core) * FAR, FAR)]
        landed(dst, ss.at[t, n], sr.at[t, n], twin)

    order = [("z", 0), ("z", 1), ("b", 0), ("c", 0), ("z", 2), ("d", 0, 0), ("d", 0, 1), ("d", 0, 2)]
    order += [("b", 1), ("c", 1), ("e", 0, 0), ("e", 0, 1), ("e", 0, 2), ("z", 3)]
    order += [("d", 1, 0), ("d", 1, 1), ("d", 1, 2), ("b", 2), ("c", 2), ("f", 0, 0), ("f", 0, 1), ("f", 0, 2)]
    order += [("e", 1, 0), ("e", 1, 1), ("e", 1, 2), ("d", 2, 0), ("d", 2, 1), ("d", 2, 2), ("b", 3), ("c", 3)]
    order += [("f", 1, 0), ("f", 1, 1), ("f", 1, 2), ("e", 2, 0), ("e", 2, 1), ("e", 2, 2)]
    order += [("d", 3, 0), ("d", 3, 1), ("d", 3, 2), ("f", 2, 0), ("f", 2, 1), ("f", 2, 2)]
    order += [("e", 3, 0), ("e", 3, 1), ("e", 3, 2), ("f", 3, 0), ("f", 3, 1), ("f", 3, 2)]
    doing = {"z": step_z1, "b": step_b, "c": step_c, "d": step_d, "e": step_e, "f": step_f}

    def run_until(*last):
        while order:
            name, *args = order.pop(0)
            doing[name](*args)
            if (name, *args) == last:
                return

    run_until("z", 1)

    head_copy = pltpu.make_async_copy(head, headbuf, lsem.at[6])
    head_copy.start()
    gain_copy = pltpu.make_async_copy(gain, gainbuf, lsem.at[7])
    gain_copy.start()
    lab_copies = [
        pltpu.make_async_copy(lab.at[:, :, cols], labels.at[:, cb], labsem.at[cb]) for cb, cols in enumerate(blocks)
    ]
    mine = [
        pltpu.make_async_copy(own(t), wts.at[t // 2, t % 2, gy], lsem.at[9 + t]) for t in range(4)
    ]

    for cb in range(4):
        landed(pad.at[0, cb, body], hs.at[0, cb], hr.at[0, cb], g_prev)
        landed(pad.at[17, cb, body], hs.at[1, cb], hr.at[1, cb], g_next)
    corner = []
    for n, plane in enumerate((0, 17)):
        corner.append(remote(pad.at[plane, :, pl.ds(128, 8)], pad.at[plane, :, above], cs.at[n, 0], cr.at[n, 0], z_next))
        corner.append(remote(pad.at[plane, :, pl.ds(8, 8)], pad.at[plane, :, below], cs.at[n, 1], cr.at[n, 1], z_prev))
    for copy in corner:
        copy.start()
    for cb in range(4):
        landed(pad.at[inner, cb, above], hs.at[2, cb], hr.at[2, cb], z_prev)
        landed(pad.at[inner, cb, below], hs.at[3, cb], hr.at[3, cb], z_next)

    @pl.when(gy == 0)
    def _():
        pad[inner, :, above] = jnp.zeros((16, 4, 8, 128), F32)

    @pl.when(gy == 3)
    def _():
        pad[inner, :, below] = jnp.zeros((16, 4, 8, 128), F32)

    xacc[...] = jnp.zeros_like(xacc)
    lane = lax.broadcasted_iota(jnp.int32, (8, 512), 1)
    not_first, not_last = lane != 0, lane != 511
    block = lax.broadcasted_iota(jnp.int32, (8, 128), 1) // 16
    low = {bit: (block // bit) % 2 == 0 for bit in (1, 2, 4)}

    def stem_row(d, i):
        totals = [[], [], []]
        for cb in range(4):
            total = [None, None, None]
            for first in range(3):
                for second in range(3):
                    x = pad[d + first, cb, pl.ds(7 + i + second, 8, stride=16), :]
                    for third in range(3):
                        term = taps[(first * 3 + second) * 3 + third] * x
                        total[third] = term if total[third] is None else total[third] + term
            for third in range(3):
                totals[third].append(total[third])
        total = [jnp.concatenate(many, axis=1) for many in totals]
        left = jnp.where(not_first, pltpu.roll(total[0], 1, 1), 0.0)
        right = jnp.where(not_last, pltpu.roll(total[2], 511, 1), 0.0)
        v = 0.5 * (total[1] + left + right)
        v = v + v * jnp.tanh(v)
        stem[d, i] = v.astype(BF16).astype(F32)

    def stem_plane(d, at):
        @pl.loop(0, 16)
        def _(i):
            stem_row(d, i)

        for upper in range(2):
            for cb in range(4):
                v = [stem[d, upper * 8 + i, :, pl.ds(cb * 128, 128)] for i in range(8)]
                for bit in (1, 2, 4):
                    for i in range(8):
                        if i & bit == 0:
                            a, b = v[i], v[i + bit]
                            v[i] = jnp.where(low[bit], a, pltpu.roll(b, bit * 16, 1))
                            v[i + bit] = jnp.where(low[bit], pltpu.roll(a, 128 - bit * 16, 1), b)
                for m in range(4):
                    pair = jnp.concatenate([v[2 * m], v[2 * m + 1]], axis=0).astype(BF16)
                    lhs[at, pl.ds(cb * 64 + m * 16, 16), pl.ds(upper * 128, 128)] = pair

    def front(g):
        base = groups[g]

        @pl.loop(0, 4)
        def _(n):
            stem_plane(base + n, n)

        embed_copy(g).wait()
        slot = g % 2

        @pl.loop(0, 4)
        def _(n):
            cols = pl.ds(pl.multiple_of(n * 256, 256), 256)
            total = xacc[:, cols]
            for part in range(4):
                total = total + jnp.dot(
                    lhs[part], embuf[slot, pl.ds(part * 256, 256), cols], preferred_element_type=F32
                )
            xacc[:, cols] = total

    volume_wait(0)
    embed_copy(1).start()
    mine[0].start()
    mine[1].start()
    front(0)
    run_until("c", 0)
    volume_wait(1)
    embed_copy(2).start()
    front(1)
    run_until("d", 0, 2)
    for copy in corner:
        copy.wait()
    volume_wait(2)
    volume_wait(3)

    @pl.when(gz == 0)
    def _():
        pad[0] = jnp.zeros((4, 144, 128), F32)

    @pl.when(gz == 31)
    def _():
        pad[17] = jnp.zeros((4, 144, 128), F32)

    for plane in (0, 17):
        @pl.when(gy == 0)
        def _():
            pad[plane, :, above] = jnp.zeros((4, 8, 128), F32)

        @pl.when(gy == 3)
        def _():
            pad[plane, :, below] = jnp.zeros((4, 8, 128), F32)

    embed_copy(3).start()
    mine[2].start()
    mine[3].start()
    for copy in lab_copies:
        copy.start()
    front(2)
    run_until("e", 0, 2)
    front(3)
    run_until("c", 2)
    gain_copy.wait()
    for t in range(4):
        mine[t].wait()

    at_row = lax.broadcasted_iota(jnp.int32, (256, 512), 0) // 8
    at_col = lax.broadcasted_iota(jnp.int32, (256, 512), 1)
    for e in range(4):
        hit = jnp.logical_and(at_col // 16 == at_row, (at_col // 4) % 4 == e)
        expand[pl.ds(e * 256, 256)] = hit.astype(F32).astype(BF16)

    def as_stored(x):
        return x.astype(BF16).astype(F32)

    @pl.loop(0, 8)
    def _(n):
        at = pl.ds(pl.multiple_of(n * 32, 32), 32)
        xacc[at] = as_stored(xacc[at])

    def mlp_up(layer, q):
        @pl.loop(0, 4)
        def _(n):
            cols = pl.ds(pl.multiple_of(n * 256, 256), 256)
            u = jnp.dot(xn[...], wts[layer, 0, q, :, cols], preferred_element_type=F32)
            hid[q, :, cols] = jax.nn.gelu(u, approximate=True).astype(BF16)

    def mlp_down(layer, q):
        @pl.loop(0, 4)
        def _(n):
            cols = pl.ds(pl.multiple_of(n * 256, 256), 256)
            xacc[:, cols] += jnp.dot(hid[q], wts[layer, 1, q, :, cols], preferred_element_type=F32)

    for layer in range(2):
        @pl.loop(0, 8)
        def _(n):
            at = pl.ds(pl.multiple_of(n * 32, 32), 32)
            x = xacc[at]
            centred = x - jnp.mean(x, -1, keepdims=True)
            spread_ = jnp.mean(centred * centred, -1, keepdims=True)
            xn[at] = (centred * lax.rsqrt(spread_ + EPS) * gainbuf[pl.ds(layer, 1)]).astype(BF16)

        mlp_up(layer, gy)
        for n in range(3):
            run_until("f", 2 * layer, n)
            mlp_up(layer, foreign[n])
        mlp_down(layer, gy)
        for n in range(3):
            run_until("f", 2 * layer + 1, n)
            mlp_down(layer, foreign[n])

        @pl.loop(0, 8)
        def _(n):
            at = pl.ds(pl.multiple_of(n * 32, 32), 32)
            xacc[at] = as_stored(xacc[at])

    head_copy.wait()
    token = lax.broadcasted_iota(jnp.int32, (256, 256), 0)
    patch = (token % 8) * 32 + token // 8
    listed = jnp.max((slots[...] == patch).astype(F32), axis=1, keepdims=True)
    q = jnp.dot(xacc[...].astype(BF16), headbuf[...], preferred_element_type=F32)
    q = (as_stored(q) * listed).T
    coarse[0] = q[:, :128]
    coarse[1] = q[:, 128:]
    token = lax.broadcasted_iota(jnp.int32, (8, 256), 1)
    own_row = (token % 8 == lax.broadcasted_iota(jnp.int32, (8, 256), 0)).astype(F32)

    for c in range(4):
        spread_q = []
        for e in range(4):
            at = pl.ds(c * 64 + e, 16, stride=4)
            part = jnp.concatenate([coarse[0, at, :], coarse[1, at, :]], axis=1)
            spread_q.append((part[:, None, :] * own_row[None]).reshape(128, 256).astype(BF16))
        u = jnp.zeros((128, 512), F32)
        for e in range(4):
            u = u + jnp.dot(spread_q[e], expand[pl.ds(e * 256, 256)], preferred_element_type=F32)
        upq[pl.ds(c * 128, 128)] = 0.5 * (u + bias[c])
    for copy in lab_copies:
        copy.wait()

    half_skip = [0.5 * skip[c] for c in range(4)]
    for cb in range(4):
        cols = pl.ds(cb * 128, 128)

        def block_step(ab, carry):
            carry = list(carry)
            a, b = lax.div(ab, 4), lax.rem(ab, 4)
            level = [upq[pl.ds(pl.multiple_of(c * 128 + ab * 8, 8), 8), cols] for c in range(4)]
            for dd in range(4):
                for ii in range(4):
                    d, i = a * 4 + dd, b * 4 + ii
                    s = stem[d, i, :, cols]
                    l = labels[d, cb, pl.ds(i, 8, stride=16), :]
                    for c in range(4):
                        t = jnp.tanh(level[c] + half_skip[c] * s)
                        carry[c] = carry[c] + t
                        match = l == c
                        carry[4 + c] = carry[4 + c] + jnp.where(match, t, 0.0)
                        carry[8 + c] = carry[8 + c] + jnp.where(match, 1.0, 0.0)
            return tuple(carry)

        final = lax.fori_loop(0, 16, block_step, (jnp.zeros((8, 128), F32),) * 12)
        for c in range(4):
            sums[pl.ds(c * 8, 8), cols] = 0.5 * (final[4 + c] + final[8 + c])
            sums[pl.ds(32 + c * 8, 8), cols] = 8 * 16 + 0.5 * final[c]
            sums[pl.ds(64 + c * 8, 8), cols] = final[8 + c]

    fold = lax.broadcasted_iota(jnp.int32, (512, 128), 0) // 16 == lax.broadcasted_iota(jnp.int32, (512, 128), 1)
    out[...] = jnp.dot(
        sums[...], fold.astype(F32), preferred_element_type=F32, precision=lax.Precision.HIGHEST
    )

    for copy in sent:
        copy.wait_send()


def per_device(
    volume, labels, patch_list, stem_kernel, embed_weight, norm_gain, up_weight, down_weight, head_weight, skip_weight, class_bias
):
    hbm = pl.BlockSpec(memory_space=pl.ANY)
    smem = pl.BlockSpec(memory_space=pltpu.SMEM)
    vmem = pl.BlockSpec(memory_space=pltpu.VMEM)
    dma = pltpu.SemaphoreType.DMA
    raw = pl.pallas_call(
        kernel,
        out_shape=jax.ShapeDtypeStruct((96, 128), F32),
        in_specs=[hbm, hbm, vmem, smem, hbm, hbm, hbm, hbm, hbm, smem, smem],
        out_specs=vmem,
        scratch_shapes=[
            pltpu.VMEM((18, 4, 144, 128), F32),
            pltpu.VMEM((2, 2, 4, 1024, 1024), BF16),
            pltpu.VMEM((2, 1024, 1024), BF16),
            pltpu.VMEM((16, 16, 8, 512), F32),
            pltpu.VMEM((16, 4, 128, 128), jnp.int32),
            pltpu.VMEM((4, 256, 256), BF16),
            pltpu.VMEM((256, 1024), F32),
            pltpu.VMEM((256, 1024), BF16),
            pltpu.VMEM((4, 256, 1024), BF16),
            pltpu.VMEM((2, 256, 128), F32),
            pltpu.VMEM((512, 512), F32),
            pltpu.VMEM((1024, 512), BF16),
            pltpu.VMEM((96, 512), F32),
            pltpu.VMEM((1024, 256), BF16),
            pltpu.VMEM((2, 1024), F32),
            dma((4, 4)), dma((4, 4)), dma((2, 2)), dma((2, 2)), dma((4, 4)), dma((4,)),
            dma((4, 2)), dma((4, 2)), dma((4, 2)), dma((4, 2)),
            dma((4, 3, 2)), dma((4, 3, 2)), dma((4, 3, 2)), dma((4, 3, 2)),
            dma((4, 3)), dma((4, 3)),
            dma((13,)),
        ],
        compiler_params=pltpu.CompilerParams(
            collective_id=0, has_side_effects=True, vmem_limit_bytes=60 * 1024 * 1024
        ),
    )(
        volume, labels, patch_list.reshape(1, 256), stem_kernel.reshape(27), embed_weight, norm_gain,
        up_weight, down_weight, head_weight, skip_weight, class_bias,
    )
    parts = raw[:, :32].reshape(3, 4, 256)
    inter, mass, count = parts[0], parts[1], parts[2]
    patch_dice = ((2.0 * inter + 1.0) / (mass + count + 1.0))[None, None]
    totals = lax.psum(jnp.sum(parts, 2), ("gz", "gy"))
    dice = (2.0 * totals[0] + 1.0) / (totals[1] + totals[2] + 1.0)
    return (patch_dice, dice)


def solution(mesh):
    placed = (
        P("gz", "gy", None),
        P("gz", "gy", None),
        P("gz", "gy", None),
        P(),
        P(),
        P(),
        P(None, None, "gy"),
        P(None, "gy", None),
        P(),
        P(),
        P(),
    )
    return jax.shard_map(
        per_device,
        mesh=mesh,
        in_specs=placed,
        out_specs=(P("gz", "gy", None, None), P()),
        check_vma=False,
    )
```

time: 757 us -> 196 us (0.26); the launches traced: 749 us -> 196 us
  local copies, waits for them, and re-layouts: 257 us -> 2.84 us
  Pallas kernels: 0 us -> 126 us
  waiting for transfers between devices: 104 us -> 0 us
  other arithmetic: 104 us -> 1.37 us
  loops' own time: 75.4 us -> 0 us
  blocking collectives: 136 us -> 65.5 us
  starting transfers between devices: 38.8 us -> 0 us
  matrix products: 19.5 us -> 0 us
  between operations: 14.3 us -> 0.64 us
    pallas_call x0 -> x1, Pallas kernels: none -> 126 us  [per_device(): pl.pallas_call(kernel, out_shape=jax.ShapeDtypeStruct((96, 128), F32), in...]
    another operation x1 -> x0, loops' own time: 75.4 us -> none  [carried_in(): return lax.fori_loop(0, count - 1, turn, so_far)]
    dynamic_slice x127 -> x0, local copies, waits for them, and re-layouts: 73.6 us -> none  [turn(): longer = join(so_far, pieces[position])]
    unnamed x1 -> x0, blocking collectives: 68.6 us -> none
    reshape x9 -> x2, local copies, waits for them, and re-layouts: 69.1 us -> 2.17 us  [the longest x1 1.29 us: per_device(): stem_kernel.reshape(27)]
    convert_element_type x6 -> x0, other arithmetic: 57.3 us -> none  [the longest x1 39.5 us: stem_field(): return jax.nn.silu(total).astype(jnp.bfloat16)]
    all_gather x2 -> x0, waiting for transfers between devices: 43.9 us -> none  [per_device(): lax.all_gather(hidden, 'gy', axis=0, tiled=True)]
    transpose x2 -> x0, local copies, waits for them, and re-layouts: 40.9 us -> none  [patch_layout(): shaped.transpose(1, 3, 0, 2, 4)]
  transfers between devices with their start and end apart: 11 -> 0, of which waited for: 6 -> 0; matrix products, arithmetic and copies ran while one was open for 32% -> 0% of each run, Pallas kernels for 0% -> 0%
where the time goes in v1:
time: 196 us
  Pallas kernels  126 us (64%)
  blocking collectives  65.5 us (33%)
  local copies, waits for them, and re-layouts  2.84 us (1%)
    pallas_call x1, Pallas kernels, per_device(): pl.pallas_call(kernel, out_shape=jax.ShapeDtypeStruct((96, 128), F32), in...  126 us
    psum x1, blocking collectives, per_device(): totals = lax.psum(jnp.sum(parts, 2), ('gz', 'gy'))  65.5 us

profile of v1, /device:TPU:1, one launch (start us, length us, event | category | flops | bytes accessed | tf_op | source)
XLA Modules:
  0.0 196.1 jit_solution(4326571865796576313)
XLA Ops:
  0.6 1.3 reshape.72.taps
  1.9 125.7 %shard_map.122 = f32[96,128]{1,0:T(8,128)} custom-call(f32[16,128,512]{2,1,0:T(8,128)} %vol.1, s32[16,128,512]{2,1,0:T(8,128)} %lab.1, s32[1,256]{1,0:T(1,128)} %bitcast.5, f32[27]{0:T(128)} %reshape.72.taps, bf16[4096,1024]{1,0:T(8,128)(2,1)} %emb.1, f32[2,1024]{1,0:T(2,128)} %gain.1, bf16[2,1024,1024]{2,1,0:T(8,128)(2,1)} %up.1, ...), custom_call_target="tpu_custom_call" | custom-call | tf_op jit(solution)/shard_map/pallas_call | solution.py:427
  127.6 0.9 reshape.73
  128.5 0.1 reduce_sum.9
  128.6 65.5 %psum.7 = f32[3,4]{1,0:T(4,128)S(1)} all-reduce(f32[3,4]{1,0:T(4,128)S(1)} %reduce_sum.9), channel_id=1, replica_groups=mesh['gz'=32,'gy'=4] {'gz','gy'}, use_global_device_ids=true, to_apply=%region_1.0 | all-reduce | flops 12 | bytes 96 | tf_op jit(solution)/shard_map/psum | solution.py:464
  194.1 0.5 fusion
  194.7 0.8 add_divide_fusion
  195.4 0.7 div.20

commit v2 on v1

--- a/solution.py
+++ b/solution.py
@@ -1,3 +1,5 @@
+import itertools
+
 import jax
 import jax.numpy as jnp
 from jax import lax
@@ -15,9 +17,9 @@
 
 def kernel(
     vol, lab, slots, taps, emb, gain, up, down, head, skip, bias,
-    out,
-    pad, wts, embuf, stem, labels, lhs, xacc, xn, hid, coarse, upq, expand, sums, headbuf, gainbuf,
-    hs, hr, cs, cr, vsem, labsem, z1s, z1r, z2s, z2r, a1s, a1r, a2s, a2r, ss, sr, lsem,
+    out, dice,
+    pad, wts, embuf, stem, labels, lhs, xacc, xn, hid, coarse, upq, expand, sums, headbuf, gainbuf, inbox, outbox,
+    hs, hr, cs, cr, vsem, labsem, z1s, z1r, z2s, z2r, a1s, a1r, a2s, a2r, ss, sr, ps, pr, lsem,
 ):
     gz, gy = lax.axis_index("gz"), lax.axis_index("gy")
     core = lax.rem(gz, 2)
@@ -37,10 +39,16 @@
     q_prev, q_next, q_far = lax.rem(gy + 3, 4), lax.rem(gy + 1, 4), lax.rem(gy + 2, 4)
     foreign = (q_prev, q_next, q_far)
 
+    inner_group = [(n, (chip * 2 + lax.rem(core + n // 4, 2), lax.rem(gy + n % 4, 4))) for n in range(1, 8)]
+    outer_group = [
+        (n, ((lax.rem(cy + n // 4, 4) * 4 + lax.rem(cx + n % 4, 4)) * 2 + core, gy)) for n in range(1, 16)
+    ]
+    crossing = (lax.rem(gz + 31 + 2 * core, 32), gy)
+
     barrier = pltpu.get_barrier_semaphore()
-    for peer in (z_next, z_prev, a_next, a_prev, g_next, g_prev, twin):
+    for _, peer in inner_group + outer_group + [(0, crossing)]:
         pl.semaphore_signal(barrier, inc=1, device_id=peer, device_id_type=MESH)
-    pl.semaphore_wait(barrier, 7)
+    pl.semaphore_wait(barrier, 23)
 
     def remote(src, dst, send, recv, peer):
         return pltpu.make_async_remote_copy(
@@ -205,18 +213,18 @@
     block = lax.broadcasted_iota(jnp.int32, (8, 128), 1) // 16
     low = {bit: (block // bit) % 2 == 0 for bit in (1, 2, 4)}
 
+    tap = {at: jnp.full((8, 128), taps[at], F32) for at in itertools.product(range(3), repeat=3)}
+
     def stem_row(d, i):
-        totals = [[], [], []]
-        for cb in range(4):
-            total = [None, None, None]
-            for first in range(3):
-                for second in range(3):
+        totals = [[None] * 4 for third in range(3)]
+        for first in range(3):
+            for second in range(3):
+                for cb in range(4):
                     x = pad[d + first, cb, pl.ds(7 + i + second, 8, stride=16), :]
                     for third in range(3):
-                        term = taps[(first * 3 + second) * 3 + third] * x
-                        total[third] = term if total[third] is None else total[third] + term
-            for third in range(3):
-                totals[third].append(total[third])
+                        term = tap[first, second, third] * x
+                        before = totals[third][cb]
+                        totals[third][cb] = term if before is None else before + term
         total = [jnp.concatenate(many, axis=1) for many in totals]
         left = jnp.where(not_first, pltpu.roll(total[0], 1, 1), 0.0)
         right = jnp.where(not_last, pltpu.roll(total[2], 511, 1), 0.0)
@@ -240,7 +248,8 @@
                             v[i + bit] = jnp.where(low[bit], pltpu.roll(a, 128 - bit * 16, 1), b)
                 for m in range(4):
                     pair = jnp.concatenate([v[2 * m], v[2 * m + 1]], axis=0).astype(BF16)
-                    lhs[at, pl.ds(cb * 64 + m * 16, 16), pl.ds(upper * 128, 128)] = pair
+                    cols = pl.ds(pl.multiple_of(at * 256 + upper * 128, 128), 128)
+                    lhs[pl.ds(cb * 64 + m * 16, 16), cols] = pair
 
     def front(g):
         base = groups[g]
@@ -252,15 +261,7 @@
         embed_copy(g).wait()
         slot = g % 2
 
-        @pl.loop(0, 4)
-        def _(n):
-            cols = pl.ds(pl.multiple_of(n * 256, 256), 256)
-            total = xacc[:, cols]
-            for part in range(4):
-                total = total + jnp.dot(
-                    lhs[part], embuf[slot, pl.ds(part * 256, 256), cols], preferred_element_type=F32
-                )
-            xacc[:, cols] = total
+        xacc[...] += jnp.dot(lhs[...], embuf[slot], preferred_element_type=F32)
 
     volume_wait(0)
     embed_copy(1).start()
@@ -322,17 +323,11 @@
         xacc[at] = as_stored(xacc[at])
 
     def mlp_up(layer, q):
-        @pl.loop(0, 4)
-        def _(n):
-            cols = pl.ds(pl.multiple_of(n * 256, 256), 256)
-            u = jnp.dot(xn[...], wts[layer, 0, q, :, cols], preferred_element_type=F32)
-            hid[q, :, cols] = jax.nn.gelu(u, approximate=True).astype(BF16)
+        u = jnp.dot(xn[...], wts[layer, 0, q], preferred_element_type=F32)
+        hid[q] = jax.nn.gelu(u, approximate=True).astype(BF16)
 
     def mlp_down(layer, q):
-        @pl.loop(0, 4)
-        def _(n):
-            cols = pl.ds(pl.multiple_of(n * 256, 256), 256)
-            xacc[:, cols] += jnp.dot(hid[q], wts[layer, 1, q, :, cols], preferred_element_type=F32)
+        xacc[...] += jnp.dot(hid[q], wts[layer, 1, q], preferred_element_type=F32)
 
     for layer in range(2):
         @pl.loop(0, 8)
@@ -360,7 +355,7 @@
     head_copy.wait()
     token = lax.broadcasted_iota(jnp.int32, (256, 256), 0)
     patch = (token % 8) * 32 + token // 8
-    listed = jnp.max((slots[...] == patch).astype(F32), axis=1, keepdims=True)
+    listed = jnp.max((slots[0] == patch).astype(F32), axis=1, keepdims=True)
     q = jnp.dot(xacc[...].astype(BF16), headbuf[...], preferred_element_type=F32)
     q = (as_stored(q) * listed).T
     coarse[0] = q[:, :128]
@@ -408,10 +403,38 @@
             sums[pl.ds(32 + c * 8, 8), cols] = 8 * 16 + 0.5 * final[c]
             sums[pl.ds(64 + c * 8, 8), cols] = final[8 + c]
 
-    fold = lax.broadcasted_iota(jnp.int32, (512, 128), 0) // 16 == lax.broadcasted_iota(jnp.int32, (512, 128), 1)
-    out[...] = jnp.dot(
-        sums[...], fold.astype(F32), preferred_element_type=F32, precision=lax.Precision.HIGHEST
+    fold = lax.broadcasted_iota(jnp.int32, (512, 256), 0) // 16 == lax.broadcasted_iota(jnp.int32, (512, 256), 1) % 32
+    folded = jnp.dot(sums[...], fold.astype(F32), preferred_element_type=F32, precision=lax.Precision.HIGHEST)
+    here = lax.broadcasted_iota(jnp.int32, (8, 256), 1) // 32 == lax.broadcasted_iota(jnp.int32, (8, 256), 0)
+    lines = [
+        jnp.sum(jnp.where(here, folded[n * 8 : n * 8 + 8], 0.0), axis=0, keepdims=True) for n in range(12)
+    ]
+    inter, mass, count = (jnp.concatenate(lines[n * 4 : n * 4 + 4], axis=0) for n in range(3))
+    out[0, 0] = (2.0 * inter + 1.0) / (mass + count + 1.0)
+
+    def send_line(x):
+        return jnp.broadcast_to(jnp.sum(x, axis=1, keepdims=True), (4, 128))
+
+    inbox[0] = jnp.concatenate(
+        [send_line(inter), send_line(mass), send_line(count), jnp.zeros((4, 128), F32)], axis=0
     )
+    for n, peer in inner_group:
+        send(inbox.at[0], inbox.at[n], ps.at[n], pr.at[n], peer)
+    for n, peer in inner_group:
+        landed(inbox.at[n], ps.at[n], pr.at[n], peer)
+    total = inbox[0]
+    for n in range(1, 8):
+        total = total + inbox[n]
+    outbox[0] = total
+    for n, peer in outer_group:
+        send(outbox.at[0], outbox.at[n], ps.at[7 + n], pr.at[7 + n], peer)
+    for n, peer in outer_group:
+        landed(outbox.at[n], ps.at[7 + n], pr.at[7 + n], peer)
+    for n in range(1, 16):
+        total = total + outbox[n]
+    ratio = (2.0 * total[0:4] + 1.0) / (total[4:8] + total[8:12] + 1.0)
+    for c in range(4):
+        dice[c] = ratio[c, 0]
 
     for copy in sent:
         copy.wait_send()
@@ -424,18 +447,18 @@
     smem = pl.BlockSpec(memory_space=pltpu.SMEM)
     vmem = pl.BlockSpec(memory_space=pltpu.VMEM)
     dma = pltpu.SemaphoreType.DMA
-    raw = pl.pallas_call(
+    return pl.pallas_call(
         kernel,
-        out_shape=jax.ShapeDtypeStruct((96, 128), F32),
+        out_shape=(jax.ShapeDtypeStruct((1, 1, 4, 256), F32), jax.ShapeDtypeStruct((4,), F32)),
         in_specs=[hbm, hbm, vmem, smem, hbm, hbm, hbm, hbm, hbm, smem, smem],
-        out_specs=vmem,
+        out_specs=(vmem, smem),
         scratch_shapes=[
             pltpu.VMEM((18, 4, 144, 128), F32),
             pltpu.VMEM((2, 2, 4, 1024, 1024), BF16),
             pltpu.VMEM((2, 1024, 1024), BF16),
             pltpu.VMEM((16, 16, 8, 512), F32),
             pltpu.VMEM((16, 4, 128, 128), jnp.int32),
-            pltpu.VMEM((4, 256, 256), BF16),
+            pltpu.VMEM((256, 1024), BF16),
             pltpu.VMEM((256, 1024), F32),
             pltpu.VMEM((256, 1024), BF16),
             pltpu.VMEM((4, 256, 1024), BF16),
@@ -445,25 +468,22 @@
             pltpu.VMEM((96, 512), F32),
             pltpu.VMEM((1024, 256), BF16),
             pltpu.VMEM((2, 1024), F32),
+            pltpu.VMEM((8, 16, 128), F32),
+            pltpu.VMEM((16, 16, 128), F32),
             dma((4, 4)), dma((4, 4)), dma((2, 2)), dma((2, 2)), dma((4, 4)), dma((4,)),
             dma((4, 2)), dma((4, 2)), dma((4, 2)), dma((4, 2)),
             dma((4, 3, 2)), dma((4, 3, 2)), dma((4, 3, 2)), dma((4, 3, 2)),
             dma((4, 3)), dma((4, 3)),
+            dma((23,)), dma((23,)),
             dma((13,)),
         ],
         compiler_params=pltpu.CompilerParams(
             collective_id=0, has_side_effects=True, vmem_limit_bytes=60 * 1024 * 1024
         ),
     )(
-        volume, labels, patch_list.reshape(1, 256), stem_kernel.reshape(27), embed_weight, norm_gain,
+        volume, labels, patch_list, stem_kernel, embed_weight, norm_gain,
         up_weight, down_weight, head_weight, skip_weight, class_bias,
     )
-    parts = raw[:, :32].reshape(3, 4, 256)
-    inter, mass, count = parts[0], parts[1], parts[2]
-    patch_dice = ((2.0 * inter + 1.0) / (mass + count + 1.0))[None, None]
-    totals = lax.psum(jnp.sum(parts, 2), ("gz", "gy"))
-    dice = (2.0 * totals[0] + 1.0) / (totals[1] + totals[2] + 1.0)
-    return (patch_dice, dice)
 
 
 def solution(mesh):

time: 196 us -> 131 us (0.67)
  blocking collectives: 65.5 us -> 0 us
    psum x1 -> x0, blocking collectives: 65.5 us -> none  [per_device(): totals = lax.psum(jnp.sum(parts, 2), ('gz', 'gy'))]
    unnamed x0 -> x2, local copies, waits for them, and re-layouts: none -> 2.4 us
    reshape x2 -> x0, local copies, waits for them, and re-layouts: 2.17 us -> none  [the longest x1 1.29 us: per_device(): stem_kernel.reshape(27)]
where the time goes in v2:
time: 131 us; the launch traced here: 130 us
  Pallas kernels  127 us (97%)
  local copies, waits for them, and re-layouts  2.4 us (2%)
    pallas_call x1, Pallas kernels, per_device(): pl.pallas_call(kernel, out_shape=(jax.ShapeDtypeStruct((1, 1, 4, 256), F3...  127 us

profile of v2, /device:TPU:1, one launch (start us, length us, event | category | flops | bytes accessed | tf_op | source)
XLA Modules:
  0.0 130.4 jit_solution(10157057714261569365)
XLA Ops:
  0.6 127.3 %shard_map.122 = (f32[1,1,4,256]{3,2,1,0:T(4,128)}, f32[4]{0:T(128)}) custom-call(f32[16,128,512]{2,1,0:T(8,128)} %vol.1, s32[16,128,512]{2,1,0:T(8,128)} %lab.1, s32[1,1,256]{2,1,0:T(1,128)} %slots.1, f32[3,3,3]{2,1,0:T(4,128)} %taps.1, bf16[4096,1024]{1,0:T(8,128)(2,1)} %emb.1, f32[2,1024]{1,0:T(2,128)} %gain.1, bf16[2,1024,1024]{2,1,0:T(8,128)(2,1)} %up.1, ...), custom_call_target="tpu_custom_call" | custom-call | tf_op jit(solution)/shard_map/pallas_call | solution.py:450
  128.0 1.3 copy.15
  129.2 1.1 copy.16

commit v3 on v2

--- a/solution.py
+++ b/solution.py
@@ -12,14 +12,15 @@
 F32 = jnp.float32
 BF16 = jnp.bfloat16
 
-NEAR, FAR, HALF = 128, 512, 64
+SIDE, PIECE, STRAIGHT = 512, 112, 64
+STAGES = ((0, 0, 0, 1024), (0, 1, 0, 1024), (1, 0, 0, 1024), (1, 1, 0, 1024))
 
 
 def kernel(
     vol, lab, slots, taps, emb, gain, up, down, head, skip, bias,
     out, dice,
-    pad, wts, embuf, stem, labels, lhs, xacc, xn, hid, coarse, upq, expand, sums, headbuf, gainbuf, inbox, outbox,
-    hs, hr, cs, cr, vsem, labsem, z1s, z1r, z2s, z2r, a1s, a1r, a2s, a2r, ss, sr, ps, pr, lsem,
+    pad, wts, embuf, stem, labels, lhs, xacc, xn, hid, coarse, upq, expand, sums, headbuf, gainbuf, edge, inbox, outbox,
+    hs, hr, cs, cr, vsem, labsem, z1s, z1r, z2s, z2r, s1s, s1r, s2s, s2r, a1s, a1r, a2s, a2r, tws, twr, ps, pr, lsem,
 ):
     gz, gy = lax.axis_index("gz"), lax.axis_index("gy")
     core = lax.rem(gz, 2)
@@ -55,6 +56,7 @@
             src_ref=src, dst_ref=dst, send_sem=send, recv_sem=recv, device_id=peer, device_id_type=MESH
         )
 
+    z1, z2, s1, s2, a1, a2, tw = (z1s, z1r), (z2s, z2r), (s1s, s1r), (s2s, s2r), (a1s, a1r), (a2s, a2r), (tws, twr)
     sent = []
 
     def send(*args):
@@ -70,11 +72,11 @@
     above, below = pl.ds(0, 8), pl.ds(136, 8)
     blocks = [pl.ds(cb * 128, 128) for cb in range(4)]
     for cb, cols in enumerate(blocks):
+        send(vol.at[:, 127, cols], edge.at[0, cb], hs.at[2, cb], hr.at[2, cb], z_next)
+        send(vol.at[:, 0, cols], edge.at[1, cb], hs.at[3, cb], hr.at[3, cb], z_prev)
+    for cb, cols in enumerate(blocks):
         send(vol.at[15, :, cols], pad.at[0, cb, body], hs.at[0, cb], hr.at[0, cb], g_next)
         send(vol.at[0, :, cols], pad.at[17, cb, body], hs.at[1, cb], hr.at[1, cb], g_prev)
-    for cb, cols in enumerate(blocks):
-        send(vol.at[:, pl.ds(120, 8), cols], pad.at[inner, cb, above], hs.at[2, cb], hr.at[2, cb], z_next)
-        send(vol.at[:, pl.ds(0, 8), cols], pad.at[inner, cb, below], hs.at[3, cb], hr.at[3, cb], z_prev)
 
     groups = (4, 8, 12, 0)
     local = []
@@ -98,82 +100,115 @@
 
     embed_copy(0).start()
 
-    def own(t):
-        return (up, down)[t % 2].at[t // 2]
-
-    def rows(which, at, offset=0, size=NEAR):
-        return pl.ds(which * FAR + at * NEAR + offset, size)
-
-    def near(t, q, at):
-        return wts.at[t // 2, t % 2, q, rows(core, at)]
-
-    def half(t, q, at, h):
-        return wts.at[t // 2, t % 2, q, rows(core, at, h * HALF, HALF)]
+    def view(t, q, at):
+        layer, matrix, first, width = STAGES[t]
+        return wts.at[layer, matrix, q, at, pl.ds(first, width)]
+
+    def own(t, at):
+        layer, matrix, first, width = STAGES[t]
+        return (up, down)[matrix].at[layer, at, pl.ds(first, width)]
 
     seed_prev, seed_next, seed_far = lax.rem(seed + 3, 4), lax.rem(seed + 1, 4), lax.rem(seed + 2, 4)
 
-    def step_z1(t):
-        piece = own(t).at[rows(core, seed)]
-        send(piece, near(t, gy, seed), z1s.at[t, 0], z1r.at[t, 0], z_next)
-        send(piece, near(t, gy, seed), z1s.at[t, 1], z1r.at[t, 1], z_prev)
+    def piece(at):
+        return pl.ds(core * SIDE + at * PIECE, PIECE)
+
+    def part(at, h, odd):
+        first = 48 if odd else 64
+        return pl.ds(core * SIDE + at * PIECE + h * first, PIECE - first if h else first)
+
+    def straight(h=None):
+        if h is None:
+            return pl.ds(core * SIDE + 4 * PIECE, STRAIGHT)
+        return pl.ds(core * SIDE + 4 * PIECE + h * (STRAIGHT // 2), STRAIGHT // 2)
+
+    def pass_on(t, q, at, sems, index, peer):
+        send(view(t, q, at), view(t, q, at), sems[0].at[index], sems[1].at[index], peer)
+
+    def await_(t, q, at, sems, index, peer):
+        landed(view(t, q, at), sems[0].at[index], sems[1].at[index], peer)
+
+    def first_z(t, at, sems):
+        send(own(t, at), view(t, gy, at), sems[0].at[t, 0], sems[1].at[t, 0], z_next)
+        send(own(t, at), view(t, gy, at), sems[0].at[t, 1], sems[1].at[t, 1], z_prev)
 
     def spread(t, n):
-        piece = near(t, foreign[n], seed)
-        send(piece, piece, a1s.at[t, n, 0], a1r.at[t, n, 0], a_next)
-        send(piece, piece, a1s.at[t, n, 1], a1r.at[t, n, 1], a_prev)
-
-    def step_b(t):
-        landed(near(t, q_prev, seed), z1s.at[t, 0], z1r.at[t, 0], z_prev)
-        piece = half(t, q_prev, seed, 0)
-        send(piece, piece, z2s.at[t, 0], z2r.at[t, 0], z_next)
-        spread(t, 0)
-        landed(near(t, q_next, seed), z1s.at[t, 1], z1r.at[t, 1], z_next)
-        piece = half(t, q_next, seed, 1)
-        send(piece, piece, z2s.at[t, 1], z2r.at[t, 1], z_prev)
-        spread(t, 1)
+        pass_on(t, foreign[n], piece(seed), a1, (t, n, 0), a_next)
+        pass_on(t, foreign[n], piece(seed), a1, (t, n, 1), a_prev)
+
+    def step_z(t):
+        first_z(t, piece(seed), z1)
+
+    def step_b(t, n):
+        peer, other = ((z_prev, z_next), (z_next, z_prev))[n]
+        await_(t, foreign[n], piece(seed), z1, (t, n), peer)
+        pass_on(t, foreign[n], part(seed, n, t % 2), z2, (t, n), other)
+        spread(t, n)
 
     def step_c(t):
-        landed(half(t, q_far, seed, 0), z2s.at[t, 0], z2r.at[t, 0], z_prev)
-        landed(half(t, q_far, seed, 1), z2s.at[t, 1], z2r.at[t, 1], z_next)
+        await_(t, q_far, part(seed, 0, t % 2), z2, (t, 0), z_prev)
+        await_(t, q_far, part(seed, 1, t % 2), z2, (t, 1), z_next)
         spread(t, 2)
 
+    def step_s(t):
+        first_z(t, straight(), s1)
+
+    def step_t(t):
+        await_(t, q_prev, straight(), s1, (t, 0), z_prev)
+        pass_on(t, q_prev, straight(0), s2, (t, 0), z_next)
+        await_(t, q_next, straight(), s1, (t, 1), z_next)
+        pass_on(t, q_next, straight(1), s2, (t, 1), z_prev)
+
+    def step_u(t):
+        await_(t, q_far, straight(0), s2, (t, 0), z_prev)
+        await_(t, q_far, straight(1), s2, (t, 1), z_next)
+
     def step_d(t, n):
-        q = foreign[n]
-        landed(near(t, q, seed_prev), a1s.at[t, n, 0], a1r.at[t, n, 0], a_prev)
-        piece = half(t, q, seed_prev, 0)
-        send(piece, piece, a2s.at[t, n, 0], a2r.at[t, n, 0], a_next)
-        landed(near(t, q, seed_next), a1s.at[t, n, 1], a1r.at[t, n, 1], a_next)
-        piece = half(t, q, seed_next, 1)
-        send(piece, piece, a2s.at[t, n, 1], a2r.at[t, n, 1], a_prev)
+        q, odd = foreign[n], (t + n) % 2
+        await_(t, q, piece(seed_prev), a1, (t, n, 0), a_prev)
+        pass_on(t, q, part(seed_prev, 0, odd), a2, (t, n, 0), a_next)
+        await_(t, q, piece(seed_next), a1, (t, n, 1), a_next)
+        pass_on(t, q, part(seed_next, 1, odd), a2, (t, n, 1), a_prev)
 
     def step_e(t, n):
-        q = foreign[n]
-        landed(half(t, q, seed_far, 0), a2s.at[t, n, 0], a2r.at[t, n, 0], a_prev)
-        landed(half(t, q, seed_far, 1), a2s.at[t, n, 1], a2r.at[t, n, 1], a_next)
-        piece = wts.at[t // 2, t % 2, q, pl.ds(core * FAR, FAR)]
-        send(piece, piece, ss.at[t, n], sr.at[t, n], twin)
+        q, odd = foreign[n], (t + n) % 2
+        await_(t, q, part(seed_far, 0, odd), a2, (t, n, 0), a_prev)
+        await_(t, q, part(seed_far, 1, odd), a2, (t, n, 1), a_next)
+        pass_on(t, q, pl.ds(core * SIDE, SIDE), tw, (t, n), twin)
 
     def step_f(t, n):
-        dst = wts.at[t // 2, t % 2, foreign[n], pl.ds((1 - core) * FAR, FAR)]
-        landed(dst, ss.at[t, n], sr.at[t, n], twin)
-
-    order = [("z", 0), ("z", 1), ("b", 0), ("c", 0), ("z", 2), ("d", 0, 0), ("d", 0, 1), ("d", 0, 2)]
-    order += [("b", 1), ("c", 1), ("e", 0, 0), ("e", 0, 1), ("e", 0, 2), ("z", 3)]
-    order += [("d", 1, 0), ("d", 1, 1), ("d", 1, 2), ("b", 2), ("c", 2), ("f", 0, 0), ("f", 0, 1), ("f", 0, 2)]
-    order += [("e", 1, 0), ("e", 1, 1), ("e", 1, 2), ("d", 2, 0), ("d", 2, 1), ("d", 2, 2), ("b", 3), ("c", 3)]
-    order += [("f", 1, 0), ("f", 1, 1), ("f", 1, 2), ("e", 2, 0), ("e", 2, 1), ("e", 2, 2)]
-    order += [("d", 3, 0), ("d", 3, 1), ("d", 3, 2), ("f", 2, 0), ("f", 2, 1), ("f", 2, 2)]
-    order += [("e", 3, 0), ("e", 3, 1), ("e", 3, 2), ("f", 3, 0), ("f", 3, 1), ("f", 3, 2)]
-    doing = {"z": step_z1, "b": step_b, "c": step_c, "d": step_d, "e": step_e, "f": step_f}
-
-    def run_until(*last):
-        while order:
-            name, *args = order.pop(0)
-            doing[name](*args)
-            if (name, *args) == last:
+        await_(t, foreign[n], pl.ds((1 - core) * SIDE, SIDE), tw, (t, n), twin)
+
+    doing = {
+        "z": step_z, "b": step_b, "c": step_c, "s": step_s, "t": step_t, "u": step_u, "d": step_d, "e": step_e, "f": step_f,
+    }
+    plan = [
+        (0.0, 'z', 0), (0.0, 'z', 1), (0.0, 's', 0), (6.3, 'b', 0, 0), (6.3, 'b', 0, 1),
+        (6.3, 'z', 2), (6.3, 's', 1), (10.0, 'd', 0, 0), (11.4, 'b', 1, 0), (11.4, 'b', 1, 1),
+        (11.4, 'z', 3), (11.4, 's', 2), (12.6, 'd', 0, 1), (14.3, 't', 0), (14.3, 'e', 0, 0),
+        (16.4, 'd', 1, 0), (16.9, 'c', 0), (17.3, 'f', 0, 0), (19.0, 'd', 1, 1), (20.2, 'e', 0, 1),
+        (22.0, 'b', 2, 0), (22.0, 'b', 2, 1), (23.2, 'f', 0, 1), (24.1, 'd', 0, 2), (24.9, 't', 1),
+        (24.9, 'e', 1, 0), (25.3, 'e', 1, 1), (27.4, 'c', 1), (27.8, 'f', 1, 0), (27.9, 'd', 2, 0),
+        (29.6, 'f', 1, 1), (30.4, 'd', 2, 1), (32.5, 'b', 3, 0), (32.5, 'b', 3, 1), (32.5, 's', 3),
+        (34.3, 'd', 1, 2), (35.4, 't', 2), (35.5, 'e', 2, 0), (36.8, 'e', 2, 1), (36.9, 'u', 0),
+        (36.9, 'e', 0, 2), (38.5, 'f', 2, 0), (39.4, 'd', 3, 0), (39.4, 'c', 2), (40.2, 'f', 2, 1),
+        (40.9, 'u', 1), (41.9, 'd', 3, 1), (42.0, 'f', 0, 2), (43.2, 'e', 1, 2), (43.4, 'c', 3),
+        (46.1, 'f', 1, 2), (46.3, 't', 3), (46.3, 'e', 3, 0), (47.0, 'd', 2, 2), (47.8, 'u', 2),
+        (48.3, 'e', 3, 1), (49.3, 'u', 3), (49.3, 'f', 3, 0), (50.8, 'd', 3, 2), (51.2, 'f', 3, 1),
+        (52.1, 'e', 2, 2), (53.4, 'e', 3, 2), (55.0, 'f', 2, 2), (56.8, 'f', 3, 2),
+    ]
+
+    done = set()
+
+    def run_until(when=None, last=None):
+        while plan and last not in done:
+            if when is not None and plan[0][0] > when:
                 return
-
-    run_until("z", 1)
+            _, *step = plan.pop(0)
+            doing[step[0]](*step[1:])
+            done.add(tuple(step))
+
+    run_until(0.0)
 
     head_copy = pltpu.make_async_copy(head, headbuf, lsem.at[6])
     head_copy.start()
@@ -183,7 +218,7 @@
         pltpu.make_async_copy(lab.at[:, :, cols], labels.at[:, cb], labsem.at[cb]) for cb, cols in enumerate(blocks)
     ]
     mine = [
-        pltpu.make_async_copy(own(t), wts.at[t // 2, t % 2, gy], lsem.at[9 + t]) for t in range(4)
+        pltpu.make_async_copy((up, down)[t % 2].at[t // 2], wts.at[t // 2, t % 2, gy], lsem.at[9 + t]) for t in range(4)
     ]
 
     for cb in range(4):
@@ -196,16 +231,13 @@
     for copy in corner:
         copy.start()
     for cb in range(4):
-        landed(pad.at[inner, cb, above], hs.at[2, cb], hr.at[2, cb], z_prev)
-        landed(pad.at[inner, cb, below], hs.at[3, cb], hr.at[3, cb], z_next)
-
-    @pl.when(gy == 0)
-    def _():
-        pad[inner, :, above] = jnp.zeros((16, 4, 8, 128), F32)
-
-    @pl.when(gy == 3)
-    def _():
-        pad[inner, :, below] = jnp.zeros((16, 4, 8, 128), F32)
+        landed(edge.at[0, cb], hs.at[2, cb], hr.at[2, cb], z_prev)
+        landed(edge.at[1, cb], hs.at[3, cb], hr.at[3, cb], z_next)
+    keep_above, keep_below = (gy > 0).astype(F32), (gy < 3).astype(F32)
+    for cb in range(4):
+        for d in range(16):
+            pad[1 + d, cb, pl.ds(7, 1)] = edge[0, cb, pl.ds(d, 1)] * keep_above
+            pad[1 + d, cb, pl.ds(136, 1)] = edge[1, cb, pl.ds(d, 1)] * keep_below
 
     xacc[...] = jnp.zeros_like(xacc)
     lane = lax.broadcasted_iota(jnp.int32, (8, 512), 1)
@@ -215,27 +247,30 @@
 
     tap = {at: jnp.full((8, 128), taps[at], F32) for at in itertools.product(range(3), repeat=3)}
 
-    def stem_row(d, i):
-        totals = [[None] * 4 for third in range(3)]
+    def stem_rows(d, first_row, many=8):
+        totals = [[[None] * 4 for third in range(3)] for _ in range(many)]
         for first in range(3):
-            for second in range(3):
+            for row in range(many + 2):
                 for cb in range(4):
-                    x = pad[d + first, cb, pl.ds(7 + i + second, 8, stride=16), :]
-                    for third in range(3):
-                        term = tap[first, second, third] * x
-                        before = totals[third][cb]
-                        totals[third][cb] = term if before is None else before + term
-        total = [jnp.concatenate(many, axis=1) for many in totals]
-        left = jnp.where(not_first, pltpu.roll(total[0], 1, 1), 0.0)
-        right = jnp.where(not_last, pltpu.roll(total[2], 511, 1), 0.0)
-        v = 0.5 * (total[1] + left + right)
-        v = v + v * jnp.tanh(v)
-        stem[d, i] = v.astype(BF16).astype(F32)
+                    x = pad[d + first, cb, pl.ds(7 + first_row + row, 8, stride=16), :]
+                    for second in range(3):
+                        if 0 <= row - second < many:
+                            mine_ = totals[row - second]
+                            for third in range(3):
+                                term = tap[first, second, third] * x
+                                mine_[third][cb] = term if mine_[third][cb] is None else mine_[third][cb] + term
+        for n in range(many):
+            total = [jnp.concatenate(blocks_, axis=1) for blocks_ in totals[n]]
+            left = jnp.where(not_first, pltpu.roll(total[0], 1, 1), 0.0)
+            right = jnp.where(not_last, pltpu.roll(total[2], 511, 1), 0.0)
+            v = 0.5 * (total[1] + left + right)
+            v = v + v * jnp.tanh(v)
+            stem[d, first_row + n] = v.astype(BF16).astype(F32)
 
     def stem_plane(d, at):
-        @pl.loop(0, 16)
-        def _(i):
-            stem_row(d, i)
+        @pl.loop(0, 2)
+        def _(n):
+            stem_rows(d, n * 8)
 
         for upper in range(2):
             for cb in range(4):
@@ -251,28 +286,29 @@
                     cols = pl.ds(pl.multiple_of(at * 256 + upper * 128, 128), 128)
                     lhs[pl.ds(cb * 64 + m * 16, 16), cols] = pair
 
-    def front(g):
+    def front(g, last):
         base = groups[g]
 
-        @pl.loop(0, 4)
-        def _(n):
-            stem_plane(base + n, n)
+        for first in (0, 2):
+            @pl.loop(first, first + 2)
+            def _(n):
+                stem_plane(base + n, n)
+
+            if first == 0:
+                run_until(last - 2.3)
 
         embed_copy(g).wait()
-        slot = g % 2
-
-        xacc[...] += jnp.dot(lhs[...], embuf[slot], preferred_element_type=F32)
+        xacc[...] += jnp.dot(lhs[...], embuf[g % 2], preferred_element_type=F32)
+        run_until(last)
 
     volume_wait(0)
     embed_copy(1).start()
     mine[0].start()
     mine[1].start()
-    front(0)
-    run_until("c", 0)
+    front(0, 8)
     volume_wait(1)
     embed_copy(2).start()
-    front(1)
-    run_until("d", 0, 2)
+    front(1, 12)
     for copy in corner:
         copy.wait()
     volume_wait(2)
@@ -300,10 +336,8 @@
     mine[3].start()
     for copy in lab_copies:
         copy.start()
-    front(2)
-    run_until("e", 0, 2)
-    front(3)
-    run_until("c", 2)
+    front(2, 16)
+    front(3, 20)
     gain_copy.wait()
     for t in range(4):
         mine[t].wait()
@@ -340,11 +374,11 @@
 
         mlp_up(layer, gy)
         for n in range(3):
-            run_until("f", 2 * layer, n)
+            run_until(last=("f", 0 if layer == 0 else 2, n))
             mlp_up(layer, foreign[n])
         mlp_down(layer, gy)
         for n in range(3):
-            run_until("f", 2 * layer + 1, n)
+            run_until(last=("f", 1 if layer == 0 else 3, n))
             mlp_down(layer, foreign[n])
 
         @pl.loop(0, 8)
@@ -436,6 +470,7 @@
     for c in range(4):
         dice[c] = ratio[c, 0]
 
+    assert not plan
     for copy in sent:
         copy.wait_send()
 
@@ -468,9 +503,11 @@
             pltpu.VMEM((96, 512), F32),
             pltpu.VMEM((1024, 256), BF16),
             pltpu.VMEM((2, 1024), F32),
+            pltpu.VMEM((2, 4, 16, 128), F32),
             pltpu.VMEM((8, 16, 128), F32),
             pltpu.VMEM((16, 16, 128), F32),
             dma((4, 4)), dma((4, 4)), dma((2, 2)), dma((2, 2)), dma((4, 4)), dma((4,)),
+            dma((4, 2)), dma((4, 2)), dma((4, 2)), dma((4, 2)),
             dma((4, 2)), dma((4, 2)), dma((4, 2)), dma((4, 2)),
             dma((4, 3, 2)), dma((4, 3, 2)), dma((4, 3, 2)), dma((4, 3, 2)),
             dma((4, 3)), dma((4, 3)),

time: 131 us -> 104 us (0.79)
  Pallas kernels: 127 us -> 100 us
    pallas_call x1, Pallas kernels: 127 us -> 100 us  [per_device(): pl.pallas_call(kernel, out_shape=(jax.ShapeDtypeStruct((1, 1, 4, 256), F3...]
where the time goes in v3:
time: 104 us; the launch traced here: 103 us
  Pallas kernels  100 us (96%)
  local copies, waits for them, and re-layouts  2.4 us (2%)
    pallas_call x1, Pallas kernels, per_device(): pl.pallas_call(kernel, out_shape=(jax.ShapeDtypeStruct((1, 1, 4, 256), F3...  100 us
    unnamed x2, local copies, waits for them, and re-layouts  2.4 us

profile of v3, /device:TPU:1, one launch (start us, length us, event | category | flops | bytes accessed | tf_op | source)
XLA Modules:
  0.0 103.4 jit_solution(16393934705203153041)
XLA Ops:
  0.6 100.4 %shard_map.122 = (f32[1,1,4,256]{3,2,1,0:T(4,128)}, f32[4]{0:T(128)}) custom-call(f32[16,128,512]{2,1,0:T(8,128)} %vol.1, s32[16,128,512]{2,1,0:T(8,128)} %lab.1, s32[1,1,256]{2,1,0:T(1,128)} %slots.1, f32[3,3,3]{2,1,0:T(4,128)} %taps.1, bf16[4096,1024]{1,0:T(8,128)(2,1)} %emb.1, f32[2,1024]{1,0:T(2,128)} %gain.1, bf16[2,1024,1024]{2,1,0:T(8,128)(2,1)} %up.1, ...), custom_call_target="tpu_custom_call" | custom-call | tf_op jit(solution)/shard_map/pallas_call | solution.py:485
  101.0 1.3 %copy.15 = f32[1,1,4,256]{3,2,1,0:T(4,128)} copy(f32[1,1,4,256]{3,2,1,0:T(4,128)} %get-tuple-element.4) | data formatting | bytes 8192
  102.3 1.1 %copy.16 = f32[4]{0:T(128)} copy(f32[4]{0:T(128)} %get-tuple-element.5) | data formatting | bytes 32

commit v4 on v3

--- a/solution.py
+++ b/solution.py
@@ -13,7 +13,7 @@
 BF16 = jnp.bfloat16
 
 SIDE, PIECE, STRAIGHT = 512, 112, 64
-STAGES = ((0, 0, 0, 1024), (0, 1, 0, 1024), (1, 0, 0, 1024), (1, 1, 0, 1024))
+STAGES = ((0, 0, 0, 512), (0, 0, 512, 512), (0, 1, 0, 512), (0, 1, 512, 512), (1, 0, 0, 512), (1, 0, 512, 512), (1, 1, 0, 512), (1, 1, 512, 512))
 
 
 def kernel(
@@ -46,38 +46,9 @@
     ]
     crossing = (lax.rem(gz + 31 + 2 * core, 32), gy)
 
-    barrier = pltpu.get_barrier_semaphore()
-    for _, peer in inner_group + outer_group + [(0, crossing)]:
-        pl.semaphore_signal(barrier, inc=1, device_id=peer, device_id_type=MESH)
-    pl.semaphore_wait(barrier, 23)
-
-    def remote(src, dst, send, recv, peer):
-        return pltpu.make_async_remote_copy(
-            src_ref=src, dst_ref=dst, send_sem=send, recv_sem=recv, device_id=peer, device_id_type=MESH
-        )
-
-    z1, z2, s1, s2, a1, a2, tw = (z1s, z1r), (z2s, z2r), (s1s, s1r), (s2s, s2r), (a1s, a1r), (a2s, a2r), (tws, twr)
-    sent = []
-
-    def send(*args):
-        copy = remote(*args)
-        copy.start()
-        sent.append(copy)
-
-    def landed(dst, send_sem, recv_sem, peer):
-        remote(dst, dst, send_sem, recv_sem, peer).wait_recv()
-
-    body = pl.ds(8, 128)
-    inner = pl.ds(1, 16)
+    body, inner = pl.ds(8, 128), pl.ds(1, 16)
     above, below = pl.ds(0, 8), pl.ds(136, 8)
     blocks = [pl.ds(cb * 128, 128) for cb in range(4)]
-    for cb, cols in enumerate(blocks):
-        send(vol.at[:, 127, cols], edge.at[0, cb], hs.at[2, cb], hr.at[2, cb], z_next)
-        send(vol.at[:, 0, cols], edge.at[1, cb], hs.at[3, cb], hr.at[3, cb], z_prev)
-    for cb, cols in enumerate(blocks):
-        send(vol.at[15, :, cols], pad.at[0, cb, body], hs.at[0, cb], hr.at[0, cb], g_next)
-        send(vol.at[0, :, cols], pad.at[17, cb, body], hs.at[1, cb], hr.at[1, cb], g_prev)
-
     groups = (4, 8, 12, 0)
     local = []
     parts = ((3, 6), (9, 4), (13, 3), (0, 3))
@@ -99,6 +70,35 @@
         )
 
     embed_copy(0).start()
+    embed_copy(1).start()
+
+    barrier = pltpu.get_barrier_semaphore()
+    for _, peer in inner_group + outer_group + [(0, crossing)]:
+        pl.semaphore_signal(barrier, inc=1, device_id=peer, device_id_type=MESH)
+    pl.semaphore_wait(barrier, 23)
+
+    def remote(src, dst, send, recv, peer):
+        return pltpu.make_async_remote_copy(
+            src_ref=src, dst_ref=dst, send_sem=send, recv_sem=recv, device_id=peer, device_id_type=MESH
+        )
+
+    z1, z2, s1, s2, a1, a2, tw = (z1s, z1r), (z2s, z2r), (s1s, s1r), (s2s, s2r), (a1s, a1r), (a2s, a2r), (tws, twr)
+    sent = []
+
+    def send(*args):
+        copy = remote(*args)
+        copy.start()
+        sent.append(copy)
+
+    def landed(dst, send_sem, recv_sem, peer):
+        remote(dst, dst, send_sem, recv_sem, peer).wait_recv()
+
+    for cb, cols in enumerate(blocks):
+        send(vol.at[:, 127, cols], edge.at[0, cb], hs.at[2, cb], hr.at[2, cb], z_next)
+        send(vol.at[:, 0, cols], edge.at[1, cb], hs.at[3, cb], hr.at[3, cb], z_prev)
+    for cb, cols in enumerate(blocks):
+        send(vol.at[15, :, cols], pad.at[0, cb, body], hs.at[0, cb], hr.at[0, cb], g_next)
+        send(vol.at[0, :, cols], pad.at[17, cb, body], hs.at[1, cb], hr.at[1, cb], g_prev)
 
     def view(t, q, at):
         layer, matrix, first, width = STAGES[t]
@@ -178,37 +178,6 @@
 
     def step_f(t, n):
         await_(t, foreign[n], pl.ds((1 - core) * SIDE, SIDE), tw, (t, n), twin)
-
-    doing = {
-        "z": step_z, "b": step_b, "c": step_c, "s": step_s, "t": step_t, "u": step_u, "d": step_d, "e": step_e, "f": step_f,
-    }
-    plan = [
-        (0.0, 'z', 0), (0.0, 'z', 1), (0.0, 's', 0), (6.3, 'b', 0, 0), (6.3, 'b', 0, 1),
-        (6.3, 'z', 2), (6.3, 's', 1), (10.0, 'd', 0, 0), (11.4, 'b', 1, 0), (11.4, 'b', 1, 1),
-        (11.4, 'z', 3), (11.4, 's', 2), (12.6, 'd', 0, 1), (14.3, 't', 0), (14.3, 'e', 0, 0),
-        (16.4, 'd', 1, 0), (16.9, 'c', 0), (17.3, 'f', 0, 0), (19.0, 'd', 1, 1), (20.2, 'e', 0, 1),
-        (22.0, 'b', 2, 0), (22.0, 'b', 2, 1), (23.2, 'f', 0, 1), (24.1, 'd', 0, 2), (24.9, 't', 1),
-        (24.9, 'e', 1, 0), (25.3, 'e', 1, 1), (27.4, 'c', 1), (27.8, 'f', 1, 0), (27.9, 'd', 2, 0),
-        (29.6, 'f', 1, 1), (30.4, 'd', 2, 1), (32.5, 'b', 3, 0), (32.5, 'b', 3, 1), (32.5, 's', 3),
-        (34.3, 'd', 1, 2), (35.4, 't', 2), (35.5, 'e', 2, 0), (36.8, 'e', 2, 1), (36.9, 'u', 0),
-        (36.9, 'e', 0, 2), (38.5, 'f', 2, 0), (39.4, 'd', 3, 0), (39.4, 'c', 2), (40.2, 'f', 2, 1),
-        (40.9, 'u', 1), (41.9, 'd', 3, 1), (42.0, 'f', 0, 2), (43.2, 'e', 1, 2), (43.4, 'c', 3),
-        (46.1, 'f', 1, 2), (46.3, 't', 3), (46.3, 'e', 3, 0), (47.0, 'd', 2, 2), (47.8, 'u', 2),
-        (48.3, 'e', 3, 1), (49.3, 'u', 3), (49.3, 'f', 3, 0), (50.8, 'd', 3, 2), (51.2, 'f', 3, 1),
-        (52.1, 'e', 2, 2), (53.4, 'e', 3, 2), (55.0, 'f', 2, 2), (56.8, 'f', 3, 2),
-    ]
-
-    done = set()
-
-    def run_until(when=None, last=None):
-        while plan and last not in done:
-            if when is not None and plan[0][0] > when:
-                return
-            _, *step = plan.pop(0)
-            doing[step[0]](*step[1:])
-            done.add(tuple(step))
-
-    run_until(0.0)
 
     head_copy = pltpu.make_async_copy(head, headbuf, lsem.at[6])
     head_copy.start()
@@ -221,23 +190,47 @@
         pltpu.make_async_copy((up, down)[t % 2].at[t // 2], wts.at[t // 2, t % 2, gy], lsem.at[9 + t]) for t in range(4)
     ]
 
-    for cb in range(4):
-        landed(pad.at[0, cb, body], hs.at[0, cb], hr.at[0, cb], g_prev)
-        landed(pad.at[17, cb, body], hs.at[1, cb], hr.at[1, cb], g_next)
     corner = []
     for n, plane in enumerate((0, 17)):
         corner.append(remote(pad.at[plane, :, pl.ds(128, 8)], pad.at[plane, :, above], cs.at[n, 0], cr.at[n, 0], z_next))
         corner.append(remote(pad.at[plane, :, pl.ds(8, 8)], pad.at[plane, :, below], cs.at[n, 1], cr.at[n, 1], z_prev))
-    for copy in corner:
-        copy.start()
-    for cb in range(4):
-        landed(edge.at[0, cb], hs.at[2, cb], hr.at[2, cb], z_prev)
-        landed(edge.at[1, cb], hs.at[3, cb], hr.at[3, cb], z_next)
-    keep_above, keep_below = (gy > 0).astype(F32), (gy < 3).astype(F32)
-    for cb in range(4):
-        for d in range(16):
-            pad[1 + d, cb, pl.ds(7, 1)] = edge[0, cb, pl.ds(d, 1)] * keep_above
-            pad[1 + d, cb, pl.ds(136, 1)] = edge[1, cb, pl.ds(d, 1)] * keep_below
+
+    def step_h(which):
+        if which == 0:
+            for cb in range(4):
+                landed(pad.at[0, cb, body], hs.at[0, cb], hr.at[0, cb], g_prev)
+                landed(pad.at[17, cb, body], hs.at[1, cb], hr.at[1, cb], g_next)
+            for copy in corner:
+                copy.start()
+        if which == 1:
+            for cb in range(4):
+                landed(edge.at[0, cb], hs.at[2, cb], hr.at[2, cb], z_prev)
+                landed(edge.at[1, cb], hs.at[3, cb], hr.at[3, cb], z_next)
+            keep_above, keep_below = (gy > 0).astype(F32), (gy < 3).astype(F32)
+            for cb in range(4):
+                for d in range(16):
+                    pad[1 + d, cb, pl.ds(7, 1)] = edge[0, cb, pl.ds(d, 1)] * keep_above
+                    pad[1 + d, cb, pl.ds(136, 1)] = edge[1, cb, pl.ds(d, 1)] * keep_below
+        if which == 2:
+            for copy in corner:
+                copy.wait()
+
+            @pl.when(gz == 0)
+            def _():
+                pad[0] = jnp.zeros((4, 144, 128), F32)
+
+            @pl.when(gz == 31)
+            def _():
+                pad[17] = jnp.zeros((4, 144, 128), F32)
+
+            for plane in (0, 17):
+                @pl.when(gy == 0)
+                def _():
+                    pad[plane, :, above] = jnp.zeros((4, 8, 128), F32)
+
+                @pl.when(gy == 3)
+                def _():
+                    pad[plane, :, below] = jnp.zeros((4, 8, 128), F32)
 
     xacc[...] = jnp.zeros_like(xacc)
     lane = lax.broadcasted_iota(jnp.int32, (8, 512), 1)
@@ -286,105 +279,105 @@
                     cols = pl.ds(pl.multiple_of(at * 256 + upper * 128, 128), 128)
                     lhs[pl.ds(cb * 64 + m * 16, 16), cols] = pair
 
-    def front(g, last):
-        base = groups[g]
-
-        for first in (0, 2):
-            @pl.loop(first, first + 2)
-            def _(n):
-                stem_plane(base + n, n)
-
-            if first == 0:
-                run_until(last - 2.3)
-
+    def step_p(k):
+        if k % 4 == 0 and k < 12:
+            volume_wait(k // 4)
+        if k == 8:
+            volume_wait(3)
+        stem_plane(groups[k // 4] + k % 4, k % 4)
+
+    def step_g(g):
         embed_copy(g).wait()
         xacc[...] += jnp.dot(lhs[...], embuf[g % 2], preferred_element_type=F32)
-        run_until(last)
-
-    volume_wait(0)
-    embed_copy(1).start()
-    mine[0].start()
-    mine[1].start()
-    front(0, 8)
-    volume_wait(1)
-    embed_copy(2).start()
-    front(1, 12)
-    for copy in corner:
-        copy.wait()
-    volume_wait(2)
-    volume_wait(3)
-
-    @pl.when(gz == 0)
-    def _():
-        pad[0] = jnp.zeros((4, 144, 128), F32)
-
-    @pl.when(gz == 31)
-    def _():
-        pad[17] = jnp.zeros((4, 144, 128), F32)
-
-    for plane in (0, 17):
-        @pl.when(gy == 0)
-        def _():
-            pad[plane, :, above] = jnp.zeros((4, 8, 128), F32)
-
-        @pl.when(gy == 3)
-        def _():
-            pad[plane, :, below] = jnp.zeros((4, 8, 128), F32)
-
-    embed_copy(3).start()
-    mine[2].start()
-    mine[3].start()
-    for copy in lab_copies:
-        copy.start()
-    front(2, 16)
-    front(3, 20)
-    gain_copy.wait()
-    for t in range(4):
-        mine[t].wait()
-
-    at_row = lax.broadcasted_iota(jnp.int32, (256, 512), 0) // 8
-    at_col = lax.broadcasted_iota(jnp.int32, (256, 512), 1)
-    for e in range(4):
-        hit = jnp.logical_and(at_col // 16 == at_row, (at_col // 4) % 4 == e)
-        expand[pl.ds(e * 256, 256)] = hit.astype(F32).astype(BF16)
+        if g < 2:
+            embed_copy(g + 2).start()
+            mine[2 * g].start()
+            mine[2 * g + 1].start()
+        if g == 1:
+            for copy in lab_copies:
+                copy.start()
 
     def as_stored(x):
         return x.astype(BF16).astype(F32)
 
-    @pl.loop(0, 8)
-    def _(n):
-        at = pl.ds(pl.multiple_of(n * 32, 32), 32)
-        xacc[at] = as_stored(xacc[at])
-
-    def mlp_up(layer, q):
-        u = jnp.dot(xn[...], wts[layer, 0, q], preferred_element_type=F32)
-        hid[q] = jax.nn.gelu(u, approximate=True).astype(BF16)
-
-    def mlp_down(layer, q):
-        xacc[...] += jnp.dot(hid[q], wts[layer, 1, q], preferred_element_type=F32)
-
-    for layer in range(2):
+    def step_n(layer):
+        if layer == 0:
+            gain_copy.wait()
+            for t in range(4):
+                mine[t].wait()
+
         @pl.loop(0, 8)
         def _(n):
             at = pl.ds(pl.multiple_of(n * 32, 32), 32)
-            x = xacc[at]
+            x = as_stored(xacc[at])
+            xacc[at] = x
             centred = x - jnp.mean(x, -1, keepdims=True)
-            spread_ = jnp.mean(centred * centred, -1, keepdims=True)
-            xn[at] = (centred * lax.rsqrt(spread_ + EPS) * gainbuf[pl.ds(layer, 1)]).astype(BF16)
-
-        mlp_up(layer, gy)
-        for n in range(3):
-            run_until(last=("f", 0 if layer == 0 else 2, n))
-            mlp_up(layer, foreign[n])
-        mlp_down(layer, gy)
-        for n in range(3):
-            run_until(last=("f", 1 if layer == 0 else 3, n))
-            mlp_down(layer, foreign[n])
-
-        @pl.loop(0, 8)
-        def _(n):
-            at = pl.ds(pl.multiple_of(n * 32, 32), 32)
-            xacc[at] = as_stored(xacc[at])
+            variance = jnp.mean(centred * centred, -1, keepdims=True)
+            xn[at] = (centred * lax.rsqrt(variance + EPS) * gainbuf[pl.ds(layer, 1)]).astype(BF16)
+
+    quarters = (*foreign, gy)
+
+    def step_up(layer, n):
+        u = jnp.dot(xn[...], wts[layer, 0, quarters[n]], preferred_element_type=F32)
+        hid[n] = jax.nn.gelu(u, approximate=True).astype(BF16)
+
+    def step_down(layer, n):
+        xacc[...] += jnp.dot(hid[n], wts[layer, 1, quarters[n]], preferred_element_type=F32)
+
+    def step_x():
+        at_row = lax.broadcasted_iota(jnp.int32, (256, 512), 0) // 8
+        at_col = lax.broadcasted_iota(jnp.int32, (256, 512), 1)
+        for e in range(4):
+            hit = jnp.logical_and(at_col // 16 == at_row, (at_col // 4) % 4 == e)
+            expand[pl.ds(e * 256, 256)] = hit.astype(F32).astype(BF16)
+
+    def step_k(cb):
+        if cb == 0:
+            for copy in lab_copies:
+                copy.wait()
+
+        def row_step(d, carry):
+            carry = list(carry)
+            for i in range(16):
+                l = labels[d, cb, pl.ds(i, 8, stride=16), :]
+                for c in range(4):
+                    carry[c] = carry[c] + jnp.where(l == c, 1.0, 0.0)
+            return tuple(carry)
+
+        final = lax.fori_loop(0, 16, row_step, (jnp.zeros((8, 128), F32),) * 4)
+        for c in range(4):
+            sums[pl.ds(64 + c * 8, 8), blocks[cb]] = final[c]
+
+    doing = {
+        "z": step_z, "b": step_b, "c": step_c, "s": step_s, "t": step_t, "u": step_u, "d": step_d, "e": step_e, "f": step_f,
+        "h": step_h, "p": step_p, "g": step_g, "n": step_n, "U": step_up, "D": step_down, "x": step_x, "k": step_k,
+    }
+    plan = [
+        ('z', 0), ('z', 1), ('s', 0), ('h', 1), ('p', 0), ('b', 0, 0), ('b', 0, 1), ('z', 2),
+        ('s', 1), ('p', 1), ('p', 2), ('p', 3), ('b', 1, 0), ('b', 1, 1), ('z', 3), ('s', 2),
+        ('g', 0), ('t', 0), ('h', 0), ('d', 0, 0), ('p', 4), ('c', 0), ('p', 5), ('d', 0, 1),
+        ('p', 6), ('p', 7), ('d', 1, 0), ('b', 2, 0), ('b', 2, 1), ('z', 4), ('s', 3), ('d', 1, 1),
+        ('t', 1), ('g', 1), ('e', 0, 0), ('p', 8), ('c', 1), ('d', 0, 2), ('p', 9), ('e', 0, 1),
+        ('h', 2), ('e', 1, 0), ('p', 10), ('b', 3, 0), ('b', 3, 1), ('z', 5), ('s', 4), ('d', 2, 0),
+        ('p', 11), ('f', 0, 0), ('t', 2), ('d', 2, 1), ('g', 2), ('u', 0), ('e', 1, 1), ('p', 12),
+        ('f', 0, 1), ('c', 2), ('d', 1, 2), ('f', 1, 0), ('p', 13), ('e', 0, 2), ('p', 14), ('d', 3, 0),
+        ('b', 4, 0), ('b', 4, 1), ('z', 6), ('s', 5), ('p', 15), ('d', 3, 1), ('f', 1, 1), ('t', 3),
+        ('e', 2, 0), ('g', 3), ('u', 1), ('e', 2, 1), ('n', 0), ('f', 0, 2), ('U', 0, 3), ('c', 3),
+        ('d', 2, 2), ('e', 1, 2), ('x',), ('e', 3, 0), ('k', 0), ('f', 2, 0), ('b', 5, 0), ('b', 5, 1),
+        ('z', 7), ('s', 6), ('d', 4, 0), ('f', 2, 1), ('k', 1), ('d', 4, 1), ('t', 4), ('e', 3, 1),
+        ('k', 2), ('u', 2), ('f', 1, 2), ('k', 3), ('d', 3, 2), ('f', 3, 0), ('c', 4), ('e', 2, 2),
+        ('U', 0, 0), ('d', 5, 0), ('U', 0, 1), ('f', 3, 1), ('b', 6, 0), ('b', 6, 1), ('d', 5, 1), ('U', 0, 2),
+        ('e', 4, 0), ('t', 5), ('e', 4, 1), ('D', 0, 3), ('f', 2, 2), ('u', 3), ('e', 3, 2), ('D', 0, 0),
+        ('D', 0, 1), ('c', 5), ('d', 4, 2), ('e', 5, 0), ('d', 6, 0), ('f', 4, 0), ('b', 7, 0), ('b', 7, 1),
+        ('s', 7), ('f', 4, 1), ('d', 6, 1), ('f', 3, 2), ('D', 0, 2), ('e', 5, 1), ('t', 6), ('n', 1),
+        ('u', 4), ('f', 5, 0), ('d', 5, 2), ('U', 1, 3), ('e', 4, 2), ('c', 6), ('e', 6, 0), ('u', 5),
+        ('U', 1, 0), ('d', 7, 0), ('c', 7), ('f', 5, 1), ('U', 1, 1), ('d', 7, 1), ('t', 7), ('e', 6, 1),
+        ('u', 6), ('e', 5, 2), ('f', 4, 2), ('f', 6, 0), ('d', 6, 2), ('e', 7, 0), ('u', 7), ('d', 7, 2),
+        ('f', 6, 1), ('e', 7, 1), ('f', 5, 2), ('U', 1, 2), ('e', 6, 2), ('D', 1, 3), ('f', 7, 0), ('D', 1, 0),
+        ('e', 7, 2), ('f', 7, 1), ('D', 1, 1), ('f', 6, 2), ('f', 7, 2), ('D', 1, 2),
+    ]
+    for name, *args in plan:
+        doing[name](*args)
 
     head_copy.wait()
     token = lax.broadcasted_iota(jnp.int32, (256, 256), 0)
@@ -407,9 +400,6 @@
         for e in range(4):
             u = u + jnp.dot(spread_q[e], expand[pl.ds(e * 256, 256)], preferred_element_type=F32)
         upq[pl.ds(c * 128, 128)] = 0.5 * (u + bias[c])
-    for copy in lab_copies:
-        copy.wait()
-
     half_skip = [0.5 * skip[c] for c in range(4)]
     for cb in range(4):
         cols = pl.ds(cb * 128, 128)
@@ -428,14 +418,12 @@
                         carry[c] = carry[c] + t
                         match = l == c
                         carry[4 + c] = carry[4 + c] + jnp.where(match, t, 0.0)
-                        carry[8 + c] = carry[8 + c] + jnp.where(match, 1.0, 0.0)
             return tuple(carry)
 
-        final = lax.fori_loop(0, 16, block_step, (jnp.zeros((8, 128), F32),) * 12)
+        final = lax.fori_loop(0, 16, block_step, (jnp.zeros((8, 128), F32),) * 8)
         for c in range(4):
-            sums[pl.ds(c * 8, 8), cols] = 0.5 * (final[4 + c] + final[8 + c])
+            sums[pl.ds(c * 8, 8), cols] = 0.5 * (final[4 + c] + sums[pl.ds(64 + c * 8, 8), cols])
             sums[pl.ds(32 + c * 8, 8), cols] = 8 * 16 + 0.5 * final[c]
-            sums[pl.ds(64 + c * 8, 8), cols] = final[8 + c]
 
     fold = lax.broadcasted_iota(jnp.int32, (512, 256), 0) // 16 == lax.broadcasted_iota(jnp.int32, (512, 256), 1) % 32
     folded = jnp.dot(sums[...], fold.astype(F32), preferred_element_type=F32, precision=lax.Precision.HIGHEST)
@@ -470,7 +458,6 @@
     for c in range(4):
         dice[c] = ratio[c, 0]
 
-    assert not plan
     for copy in sent:
         copy.wait_send()
 
@@ -507,10 +494,10 @@
             pltpu.VMEM((8, 16, 128), F32),
             pltpu.VMEM((16, 16, 128), F32),
             dma((4, 4)), dma((4, 4)), dma((2, 2)), dma((2, 2)), dma((4, 4)), dma((4,)),
-            dma((4, 2)), dma((4, 2)), dma((4, 2)), dma((4, 2)),
-            dma((4, 2)), dma((4, 2)), dma((4, 2)), dma((4, 2)),
-            dma((4, 3, 2)), dma((4, 3, 2)), dma((4, 3, 2)), dma((4, 3, 2)),
-            dma((4, 3)), dma((4, 3)),
+            dma((8, 2)), dma((8, 2)), dma((8, 2)), dma((8, 2)),
+            dma((8, 2)), dma((8, 2)), dma((8, 2)), dma((8, 2)),
+            dma((8, 3, 2)), dma((8, 3, 2)), dma((8, 3, 2)), dma((8, 3, 2)),
+            dma((8, 3)), dma((8, 3)),
             dma((23,)), dma((23,)),
             dma((13,)),
         ],

time: 104 us -> 94.4 us (0.908)
  Pallas kernels: 100 us -> 90.9 us
    pallas_call x1, Pallas kernels: 100 us -> 90.9 us  [per_device(): pl.pallas_call(kernel, out_shape=(jax.ShapeDtypeStruct((1, 1, 4, 256), F3...]
where the time goes in v4:
time: 94.4 us; the launch traced here: 93.9 us
  Pallas kernels  90.9 us (96%)
  local copies, waits for them, and re-layouts  2.4 us (3%)
    pallas_call x1, Pallas kernels, per_device(): pl.pallas_call(kernel, out_shape=(jax.ShapeDtypeStruct((1, 1, 4, 256), F3...  90.9 us
    unnamed x2, local copies, waits for them, and re-layouts  2.4 us

profile of v4, /device:TPU:1, one launch (start us, length us, event | category | flops | bytes accessed | tf_op | source)
XLA Modules:
  0.0 93.9 jit_solution(13941749182573926269)
XLA Ops:
  0.6 90.9 %shard_map.122 = (f32[1,1,4,256]{3,2,1,0:T(4,128)}, f32[4]{0:T(128)}) custom-call(f32[16,128,512]{2,1,0:T(8,128)} %vol.1, s32[16,128,512]{2,1,0:T(8,128)} %lab.1, s32[1,1,256]{2,1,0:T(1,128)} %slots.1, f32[3,3,3]{2,1,0:T(4,128)} %taps.1, bf16[4096,1024]{1,0:T(8,128)(2,1)} %emb.1, f32[2,1024]{1,0:T(2,128)} %gain.1, bf16[2,1024,1024]{2,1,0:T(8,128)(2,1)} %up.1, ...), custom_call_target="tpu_custom_call" | custom-call | tf_op jit(solution)/shard_map/pallas_call | solution.py:472
  91.5 1.3 %copy.15 = f32[1,1,4,256]{3,2,1,0:T(4,128)} copy(f32[1,1,4,256]{3,2,1,0:T(4,128)} %get-tuple-element.4) | data formatting | bytes 8192
  92.8 1.1 %copy.16 = f32[4]{0:T(128)} copy(f32[4]{0:T(128)} %get-tuple-element.5) | data formatting | bytes 32

commit v5 on v4

--- a/solution.py
+++ b/solution.py
@@ -13,13 +13,13 @@
 BF16 = jnp.bfloat16
 
 SIDE, PIECE, STRAIGHT = 512, 112, 64
-STAGES = ((0, 0, 0, 512), (0, 0, 512, 512), (0, 1, 0, 512), (0, 1, 512, 512), (1, 0, 0, 512), (1, 0, 512, 512), (1, 1, 0, 512), (1, 1, 512, 512))
+STAGES = ((0, 0, 0, 512), (0, 0, 512, 512), (0, 1, 0, 512), (0, 1, 512, 512), (1, 0, 0, 512), (1, 0, 512, 512), (1, 1, 0, 256))
 
 
 def kernel(
     vol, lab, slots, taps, emb, gain, up, down, head, skip, bias,
     out, dice,
-    pad, wts, embuf, stem, labels, lhs, xacc, xn, hid, coarse, upq, expand, sums, headbuf, gainbuf, edge, inbox, outbox,
+    pad, wts, embuf, stem, labels, lhs, xacc, xn, hid, coarse, upq, expand, sums, headbuf, gainbuf, edge, cacc, inbox, outbox,
     hs, hr, cs, cr, vsem, labsem, z1s, z1r, z2s, z2r, s1s, s1r, s2s, s2r, a1s, a1r, a2s, a2r, tws, twr, ps, pr, lsem,
 ):
     gz, gy = lax.axis_index("gz"), lax.axis_index("gy")
@@ -69,6 +69,12 @@
             emb.at[pl.ds(groups[g] * 256, 1024)], embuf.at[g % 2], lsem.at[4 + g % 2]
         )
 
+    mine = [
+        pltpu.make_async_copy((up, down)[t % 2].at[t // 2], wts.at[t // 2, t % 2, gy], lsem.at[9 + t]) for t in range(4)
+    ]
+    head_copy = pltpu.make_async_copy(head, headbuf, lsem.at[6])
+    head_copy.start()
+    mine[3].start()
     embed_copy(0).start()
     embed_copy(1).start()
 
@@ -106,6 +112,8 @@
 
     def own(t, at):
         layer, matrix, first, width = STAGES[t]
+        if (layer, matrix) == (1, 1):
+            return wts.at[layer, matrix, gy, at, pl.ds(first, width)]
         return (up, down)[matrix].at[layer, at, pl.ds(first, width)]
 
     seed_prev, seed_next, seed_far = lax.rem(seed + 3, 4), lax.rem(seed + 1, 4), lax.rem(seed + 2, 4)
@@ -179,17 +187,11 @@
     def step_f(t, n):
         await_(t, foreign[n], pl.ds((1 - core) * SIDE, SIDE), tw, (t, n), twin)
 
-    head_copy = pltpu.make_async_copy(head, headbuf, lsem.at[6])
-    head_copy.start()
     gain_copy = pltpu.make_async_copy(gain, gainbuf, lsem.at[7])
     gain_copy.start()
     lab_copies = [
         pltpu.make_async_copy(lab.at[:, :, cols], labels.at[:, cb], labsem.at[cb]) for cb, cols in enumerate(blocks)
     ]
-    mine = [
-        pltpu.make_async_copy((up, down)[t % 2].at[t // 2], wts.at[t // 2, t % 2, gy], lsem.at[9 + t]) for t in range(4)
-    ]
-
     corner = []
     for n, plane in enumerate((0, 17)):
         corner.append(remote(pad.at[plane, :, pl.ds(128, 8)], pad.at[plane, :, above], cs.at[n, 0], cr.at[n, 0], z_next))
@@ -292,7 +294,8 @@
         if g < 2:
             embed_copy(g + 2).start()
             mine[2 * g].start()
-            mine[2 * g + 1].start()
+        if g == 0:
+            mine[1].start()
         if g == 1:
             for copy in lab_copies:
                 copy.start()
@@ -303,7 +306,7 @@
     def step_n(layer):
         if layer == 0:
             gain_copy.wait()
-            for t in range(4):
+            for t in range(3):
                 mine[t].wait()
 
         @pl.loop(0, 8)
@@ -315,13 +318,25 @@
             variance = jnp.mean(centred * centred, -1, keepdims=True)
             xn[at] = (centred * lax.rsqrt(variance + EPS) * gainbuf[pl.ds(layer, 1)]).astype(BF16)
 
+        if layer == 1:
+            cacc[...] = jnp.dot(xacc[...].astype(BF16), headbuf[...], preferred_element_type=F32)
+
     quarters = (*foreign, gy)
 
     def step_up(layer, n):
         u = jnp.dot(xn[...], wts[layer, 0, quarters[n]], preferred_element_type=F32)
         hid[n] = jax.nn.gelu(u, approximate=True).astype(BF16)
 
+    def step_w():
+        mine[3].wait()
+        head_copy.wait()
+        folded_rows = jnp.dot(wts[1, 1, gy], headbuf[...], preferred_element_type=F32)
+        wts[1, 1, gy, :, pl.ds(0, 256)] = folded_rows.astype(BF16)
+
     def step_down(layer, n):
+        if layer == 1:
+            cacc[...] += jnp.dot(hid[n], wts[1, 1, quarters[n], :, pl.ds(0, 256)], preferred_element_type=F32)
+            return
         xacc[...] += jnp.dot(hid[n], wts[layer, 1, quarters[n]], preferred_element_type=F32)
 
     def step_x():
@@ -340,6 +355,7 @@
             carry = list(carry)
             for i in range(16):
                 l = labels[d, cb, pl.ds(i, 8, stride=16), :]
+                pad[d, cb, pl.ds(i * 8, 8)] = l.astype(F32)
                 for c in range(4):
                     carry[c] = carry[c] + jnp.where(l == c, 1.0, 0.0)
             return tuple(carry)
@@ -350,41 +366,37 @@
 
     doing = {
         "z": step_z, "b": step_b, "c": step_c, "s": step_s, "t": step_t, "u": step_u, "d": step_d, "e": step_e, "f": step_f,
-        "h": step_h, "p": step_p, "g": step_g, "n": step_n, "U": step_up, "D": step_down, "x": step_x, "k": step_k,
+        "h": step_h, "p": step_p, "g": step_g, "n": step_n, "U": step_up, "D": step_down, "x": step_x, "w": step_w, "k": step_k,
     }
     plan = [
-        ('z', 0), ('z', 1), ('s', 0), ('h', 1), ('p', 0), ('b', 0, 0), ('b', 0, 1), ('z', 2),
-        ('s', 1), ('p', 1), ('p', 2), ('p', 3), ('b', 1, 0), ('b', 1, 1), ('z', 3), ('s', 2),
-        ('g', 0), ('t', 0), ('h', 0), ('d', 0, 0), ('p', 4), ('c', 0), ('p', 5), ('d', 0, 1),
-        ('p', 6), ('p', 7), ('d', 1, 0), ('b', 2, 0), ('b', 2, 1), ('z', 4), ('s', 3), ('d', 1, 1),
-        ('t', 1), ('g', 1), ('e', 0, 0), ('p', 8), ('c', 1), ('d', 0, 2), ('p', 9), ('e', 0, 1),
-        ('h', 2), ('e', 1, 0), ('p', 10), ('b', 3, 0), ('b', 3, 1), ('z', 5), ('s', 4), ('d', 2, 0),
-        ('p', 11), ('f', 0, 0), ('t', 2), ('d', 2, 1), ('g', 2), ('u', 0), ('e', 1, 1), ('p', 12),
-        ('f', 0, 1), ('c', 2), ('d', 1, 2), ('f', 1, 0), ('p', 13), ('e', 0, 2), ('p', 14), ('d', 3, 0),
-        ('b', 4, 0), ('b', 4, 1), ('z', 6), ('s', 5), ('p', 15), ('d', 3, 1), ('f', 1, 1), ('t', 3),
-        ('e', 2, 0), ('g', 3), ('u', 1), ('e', 2, 1), ('n', 0), ('f', 0, 2), ('U', 0, 3), ('c', 3),
-        ('d', 2, 2), ('e', 1, 2), ('x',), ('e', 3, 0), ('k', 0), ('f', 2, 0), ('b', 5, 0), ('b', 5, 1),
-        ('z', 7), ('s', 6), ('d', 4, 0), ('f', 2, 1), ('k', 1), ('d', 4, 1), ('t', 4), ('e', 3, 1),
-        ('k', 2), ('u', 2), ('f', 1, 2), ('k', 3), ('d', 3, 2), ('f', 3, 0), ('c', 4), ('e', 2, 2),
-        ('U', 0, 0), ('d', 5, 0), ('U', 0, 1), ('f', 3, 1), ('b', 6, 0), ('b', 6, 1), ('d', 5, 1), ('U', 0, 2),
-        ('e', 4, 0), ('t', 5), ('e', 4, 1), ('D', 0, 3), ('f', 2, 2), ('u', 3), ('e', 3, 2), ('D', 0, 0),
-        ('D', 0, 1), ('c', 5), ('d', 4, 2), ('e', 5, 0), ('d', 6, 0), ('f', 4, 0), ('b', 7, 0), ('b', 7, 1),
-        ('s', 7), ('f', 4, 1), ('d', 6, 1), ('f', 3, 2), ('D', 0, 2), ('e', 5, 1), ('t', 6), ('n', 1),
-        ('u', 4), ('f', 5, 0), ('d', 5, 2), ('U', 1, 3), ('e', 4, 2), ('c', 6), ('e', 6, 0), ('u', 5),
-        ('U', 1, 0), ('d', 7, 0), ('c', 7), ('f', 5, 1), ('U', 1, 1), ('d', 7, 1), ('t', 7), ('e', 6, 1),
-        ('u', 6), ('e', 5, 2), ('f', 4, 2), ('f', 6, 0), ('d', 6, 2), ('e', 7, 0), ('u', 7), ('d', 7, 2),
-        ('f', 6, 1), ('e', 7, 1), ('f', 5, 2), ('U', 1, 2), ('e', 6, 2), ('D', 1, 3), ('f', 7, 0), ('D', 1, 0),
-        ('e', 7, 2), ('f', 7, 1), ('D', 1, 1), ('f', 6, 2), ('f', 7, 2), ('D', 1, 2),
+        ('z', 0), ('z', 1), ('w',), ('h', 1), ('p', 0), ('b', 0, 0), ('b', 0, 1), ('z', 2),
+        ('s', 0), ('p', 1), ('p', 2), ('p', 3), ('b', 1, 0), ('b', 1, 1), ('z', 3), ('s', 1),
+        ('g', 0), ('h', 0), ('p', 4), ('d', 0, 0), ('c', 0), ('p', 5), ('d', 0, 1), ('p', 6),
+        ('b', 2, 0), ('b', 2, 1), ('z', 4), ('s', 2), ('d', 1, 0), ('p', 7), ('t', 0), ('d', 1, 1),
+        ('g', 1), ('e', 0, 0), ('c', 1), ('p', 8), ('d', 0, 2), ('p', 9), ('e', 0, 1), ('h', 2),
+        ('p', 10), ('b', 3, 0), ('b', 3, 1), ('z', 5), ('s', 3), ('d', 2, 0), ('p', 11), ('f', 0, 0),
+        ('t', 1), ('d', 2, 1), ('e', 1, 0), ('g', 2), ('c', 2), ('e', 1, 1), ('p', 12), ('f', 0, 1),
+        ('d', 1, 2), ('p', 13), ('b', 4, 0), ('b', 4, 1), ('z', 6), ('s', 4), ('p', 14), ('d', 3, 0),
+        ('f', 1, 0), ('p', 15), ('t', 2), ('d', 3, 1), ('f', 1, 1), ('u', 0), ('e', 0, 2), ('e', 2, 0),
+        ('g', 3), ('e', 2, 1), ('c', 3), ('n', 0), ('U', 0, 3), ('d', 2, 2), ('x',), ('b', 5, 0),
+        ('b', 5, 1), ('k', 0), ('d', 4, 0), ('f', 0, 2), ('k', 1), ('t', 3), ('f', 2, 0), ('d', 4, 1),
+        ('u', 1), ('e', 1, 2), ('e', 3, 0), ('f', 2, 1), ('k', 2), ('e', 3, 1), ('c', 4), ('k', 3),
+        ('d', 3, 2), ('b', 6, 0), ('b', 6, 1), ('s', 5), ('s', 6), ('U', 0, 0), ('d', 5, 0), ('t', 4),
+        ('U', 0, 1), ('f', 1, 2), ('u', 2), ('e', 2, 2), ('f', 3, 0), ('d', 5, 1), ('U', 0, 2), ('e', 4, 0),
+        ('c', 5), ('f', 3, 1), ('e', 4, 1), ('u', 3), ('D', 0, 3), ('c', 6), ('D', 0, 0), ('d', 4, 2),
+        ('e', 3, 2), ('D', 0, 1), ('t', 5), ('d', 6, 0), ('f', 2, 2), ('t', 6), ('d', 6, 1), ('u', 4),
+        ('e', 5, 0), ('f', 4, 0), ('e', 5, 1), ('f', 4, 1), ('d', 5, 2), ('f', 3, 2), ('D', 0, 2), ('d', 6, 2),
+        ('u', 5), ('n', 1), ('u', 6), ('e', 4, 2), ('e', 6, 0), ('e', 6, 1), ('U', 1, 3), ('f', 5, 0),
+        ('U', 1, 0), ('f', 5, 1), ('e', 5, 2), ('U', 1, 1), ('e', 6, 2), ('f', 4, 2), ('f', 6, 0), ('f', 6, 1),
+        ('f', 5, 2), ('U', 1, 2), ('f', 6, 2), ('D', 1, 3), ('D', 1, 0), ('D', 1, 1), ('D', 1, 2),
     ]
     for name, *args in plan:
         doing[name](*args)
 
-    head_copy.wait()
     token = lax.broadcasted_iota(jnp.int32, (256, 256), 0)
     patch = (token % 8) * 32 + token // 8
     listed = jnp.max((slots[0] == patch).astype(F32), axis=1, keepdims=True)
-    q = jnp.dot(xacc[...].astype(BF16), headbuf[...], preferred_element_type=F32)
-    q = (as_stored(q) * listed).T
+    q = (as_stored(cacc[...]) * listed).T
     coarse[0] = q[:, :128]
     coarse[1] = q[:, 128:]
     token = lax.broadcasted_iota(jnp.int32, (8, 256), 1)
@@ -412,11 +424,11 @@
                 for ii in range(4):
                     d, i = a * 4 + dd, b * 4 + ii
                     s = stem[d, i, :, cols]
-                    l = labels[d, cb, pl.ds(i, 8, stride=16), :]
+                    l = pad[d, cb, pl.ds(pl.multiple_of(i * 8, 8), 8)]
                     for c in range(4):
                         t = jnp.tanh(level[c] + half_skip[c] * s)
                         carry[c] = carry[c] + t
-                        match = l == c
+                        match = l == float(c)
                         carry[4 + c] = carry[4 + c] + jnp.where(match, t, 0.0)
             return tuple(carry)
 
@@ -432,8 +444,6 @@
         jnp.sum(jnp.where(here, folded[n * 8 : n * 8 + 8], 0.0), axis=0, keepdims=True) for n in range(12)
     ]
     inter, mass, count = (jnp.concatenate(lines[n * 4 : n * 4 + 4], axis=0) for n in range(3))
-    out[0, 0] = (2.0 * inter + 1.0) / (mass + count + 1.0)
-
     def send_line(x):
         return jnp.broadcast_to(jnp.sum(x, axis=1, keepdims=True), (4, 128))
 
@@ -442,6 +452,10 @@
     )
     for n, peer in inner_group:
         send(inbox.at[0], inbox.at[n], ps.at[n], pr.at[n], peer)
+    for copy in sent:
+        copy.wait_send()
+    sent.clear()
+    out[0, 0] = (2.0 * inter + 1.0) / (mass + count + 1.0)
     for n, peer in inner_group:
         landed(inbox.at[n], ps.at[n], pr.at[n], peer)
     total = inbox[0]
@@ -452,14 +466,13 @@
         send(outbox.at[0], outbox.at[n], ps.at[7 + n], pr.at[7 + n], peer)
     for n, peer in outer_group:
         landed(outbox.at[n], ps.at[7 + n], pr.at[7 + n], peer)
+    for copy in sent:
+        copy.wait_send()
     for n in range(1, 16):
         total = total + outbox[n]
     ratio = (2.0 * total[0:4] + 1.0) / (total[4:8] + total[8:12] + 1.0)
     for c in range(4):
         dice[c] = ratio[c, 0]
-
-    for copy in sent:
-        copy.wait_send()
 
 
 def per_device(
@@ -491,13 +504,14 @@
             pltpu.VMEM((1024, 256), BF16),
             pltpu.VMEM((2, 1024), F32),
             pltpu.VMEM((2, 4, 16, 128), F32),
+            pltpu.VMEM((256, 256), F32),
             pltpu.VMEM((8, 16, 128), F32),
             pltpu.VMEM((16, 16, 128), F32),
             dma((4, 4)), dma((4, 4)), dma((2, 2)), dma((2, 2)), dma((4, 4)), dma((4,)),
-            dma((8, 2)), dma((8, 2)), dma((8, 2)), dma((8, 2)),
-            dma((8, 2)), dma((8, 2)), dma((8, 2)), dma((8, 2)),
-            dma((8, 3, 2)), dma((8, 3, 2)), dma((8, 3, 2)), dma((8, 3, 2)),
-            dma((8, 3)), dma((8, 3)),
+            dma((7, 2)), dma((7, 2)), dma((7, 2)), dma((7, 2)),
+            dma((7, 2)), dma((7, 2)), dma((7, 2)), dma((7, 2)),
+            dma((7, 3, 2)), dma((7, 3, 2)), dma((7, 3, 2)), dma((7, 3, 2)),
+            dma((7, 3)), dma((7, 3)),
             dma((23,)), dma((23,)),
             dma((13,)),
         ],

time: 94.4 us -> 84.6 us (0.90)
  Pallas kernels: 90.9 us -> 81.4 us
    pallas_call x1, Pallas kernels: 90.9 us -> 81.4 us  [per_device(): pl.pallas_call(kernel, out_shape=(jax.ShapeDtypeStruct((1, 1, 4, 256), F3...]
where the time goes in v5:
time: 84.6 us; the launch traced here: 84.4 us
  Pallas kernels  81.4 us (96%)
  local copies, waits for them, and re-layouts  2.4 us (3%)
    pallas_call x1, Pallas kernels, per_device(): pl.pallas_call(kernel, out_shape=(jax.ShapeDtypeStruct((1, 1, 4, 256), F3...  81.4 us
    unnamed x2, local copies, waits for them, and re-layouts  2.4 us

profile of v5, /device:TPU:1, one launch (start us, length us, event | category | flops | bytes accessed | tf_op | source)
XLA Modules:
  0.0 84.4 jit_solution(4835244206408610137)
XLA Ops:
  0.6 81.4 %shard_map.122 = (f32[1,1,4,256]{3,2,1,0:T(4,128)}, f32[4]{0:T(128)}) custom-call(f32[16,128,512]{2,1,0:T(8,128)} %vol.1, s32[16,128,512]{2,1,0:T(8,128)} %lab.1, s32[1,1,256]{2,1,0:T(1,128)} %slots.1, f32[3,3,3]{2,1,0:T(4,128)} %taps.1, bf16[4096,1024]{1,0:T(8,128)(2,1)} %emb.1, f32[2,1024]{1,0:T(2,128)} %gain.1, bf16[2,1024,1024]{2,1,0:T(8,128)(2,1)} %up.1, ...), custom_call_target="tpu_custom_call" | custom-call | tf_op jit(solution)/shard_map/pallas_call | solution.py:485
  82.0 1.3 %copy.15 = f32[1,1,4,256]{3,2,1,0:T(4,128)} copy(f32[1,1,4,256]{3,2,1,0:T(4,128)} %get-tuple-element.4) | data formatting | bytes 8192
  83.3 1.1 %copy.16 = f32[4]{0:T(128)} copy(f32[4]{0:T(128)} %get-tuple-element.5) | data formatting | bytes 32
